TPU v7x, 128 devices: a whole 4x4x4 slice. The times are simulated.
128 devices in a mesh: dp: 8 (over y_lo, z), ctx: 8 (over x, y_hi), tp: 2 (over core).
Axes of the slice: x: 4, y: 4 (y_hi: 2, y_lo: 2; y = y_hi * 2 + y_lo), z: 4, core: 2. Of those that a mesh axis runs over, the one named last changes fastest.
Arguments:
- block_input: bfloat16 [8192, 2048], P(('dp', 'ctx')), may hold values from -6 to 6
- out_cotangent: bfloat16 [8192, 2048], P(('dp', 'ctx')), may hold values from -6 to 6
- token_order: int32 [8, 1024], P('dp', 'ctx'), may hold values from 0 to 1023, each once within a row
- seq_lengths: int32 [8, 4], P('dp'), may hold values from 1 to 768, 1024 in all within a row
- w_qkv: float32 [2048, 3, 2048], P(('dp', 'ctx'), None, 'tp'), may hold values from -0.125 to 0.125
- w_out: float32 [2, 1024, 2048], P('tp', ('dp', 'ctx')), may hold values from -1 to 1
- w_fc1: float32 [2048, 8192], P(('dp', 'ctx'), 'tp'), may hold values from -0.125 to 0.125
- w_fc2: float32 [2, 4096, 2048], P('tp', ('dp', 'ctx')), may hold values from -0.0625 to 0.0625
- vectors: float32 [11, 2048], replicated, may hold values from -0.9 to 1.3, as said below
- mom1_qkv: float32 [2048, 3, 2048], P(('dp', 'ctx'), None, 'tp'), may hold values from -32 to 32
- mom1_out: float32 [2, 1024, 2048], P('tp', ('dp', 'ctx')), may hold values from -4 to 4
- mom1_fc1: float32 [2048, 8192], P(('dp', 'ctx'), 'tp'), may hold values from -16 to 16
- mom1_fc2: float32 [2, 4096, 2048], P('tp', ('dp', 'ctx')), may hold values from -32 to 32
- mom1_vec: float32 [11, 2048], replicated, may hold values from -64 to 64
- mom2_qkv: float32 [2048, 3, 2048], P(('dp', 'ctx'), None, 'tp'), may hold values from 54.0672 to 860.16
- mom2_out: float32 [2, 1024, 2048], P('tp', ('dp', 'ctx')), may hold values from 3.328 to 53.76
- mom2_fc1: float32 [2048, 8192], P(('dp', 'ctx'), 'tp'), may hold values from 13.1072 to 212.992
- mom2_fc2: float32 [2, 4096, 2048], P('tp', ('dp', 'ctx')), may hold values from 77.0048 to 1228.8
- mom2_vec: float32 [11, 2048], replicated, may hold values from 212.992 to 3440.64
Outputs:
- block_output: bfloat16 [8192, 2048], P(('dp', 'ctx'))
- input_grad: float32 [8192, 2048], P(('dp', 'ctx'))
- new_w_qkv: float32 [2048, 3, 2048], P(('dp', 'ctx'), None, 'tp')
- new_w_out: float32 [2, 1024, 2048], P('tp', ('dp', 'ctx'))
- new_w_fc1: float32 [2048, 8192], P(('dp', 'ctx'), 'tp')
- new_w_fc2: float32 [2, 4096, 2048], P('tp', ('dp', 'ctx'))
- new_vectors: float32 [11, 2048], replicated
- new_mom1_qkv: float32 [2048, 3, 2048], P(('dp', 'ctx'), None, 'tp')
- new_mom1_out: float32 [2, 1024, 2048], P('tp', ('dp', 'ctx'))
- new_mom1_fc1: float32 [2048, 8192], P(('dp', 'ctx'), 'tp')
- new_mom1_fc2: float32 [2, 4096, 2048], P('tp', ('dp', 'ctx'))
- new_mom1_vec: float32 [11, 2048], replicated
- new_mom2_qkv: float32 [2048, 3, 2048], P(('dp', 'ctx'), None, 'tp')
- new_mom2_out: float32 [2, 1024, 2048], P('tp', ('dp', 'ctx'))
- new_mom2_fc1: float32 [2048, 8192], P(('dp', 'ctx'), 'tp')
- new_mom2_fc2: float32 [2, 4096, 2048], P('tp', ('dp', 'ctx'))
- new_mom2_vec: float32 [11, 2048], replicated
Inputs may be any that keep to these rules, and one draw needn't show every extreme that they name: `token_order`: each row holds every number of 0 to 1023 once. `seq_lengths`: each row sums to 1024; its largest entry is 768. `vectors`: row 9 lies near one.
All inputs are finite; a program needn't handle non-finite values.
Results may differ from a plain program's by a relative error of at most 0.02.
Values may be sent and summed in bfloat16 or wider, within the bound.
No kernel may reach another device: no remote copies, remote signals or barrier semaphores. Data moves between devices by JAX's collectives and lax.ppermute only.
A program may use at most 256 MiB of HBM per device.

v0:
```python
from functools import partial
import math

import jax
import jax.numpy as jnp
from jax import lax
from jax.sharding import PartitionSpec as P

D = 2048
FF = 8192
HD = 64
ROT = 32
STEP = 10


NORM_EPS = 1e-05
SCORE_SCALE = 0.125
MASKED = -1e30
ROPE_BASE = 10000.0
BETA_ONE = 0.9
BETA_TWO = 0.95
ADAM_EPS = 1e-08
WEIGHT_DECAY = 0.1


def shifted(value, axis, steps):
    count = lax.axis_size(axis)
    pairs = [(source, (source + steps) % count) for source in range(count)]
    return lax.ppermute(value, axis, pairs)


def places(order_row, length_row):
    seq_ends = jnp.cumsum(length_row)
    seq_starts = seq_ends - length_row
    inside = (order_row[:, None] >= seq_starts[None, :]) & (order_row[:, None] < seq_ends[None, :])
    doc_ids = jnp.sum((order_row[:, None] >= seq_ends[None, :]).astype(jnp.int32), axis=1)
    seq_first = jnp.sum(jnp.where(inside, seq_starts[None, :], 0), axis=1)
    return (doc_ids, order_row - seq_first)


def angles(positions):
    half_rot = ROT // 2
    inverse = ROPE_BASE ** (-(2.0 * jnp.arange(half_rot, dtype=jnp.float32)) / ROT)
    rotation = positions.astype(jnp.float32)[:, None] * inverse[None, :]
    return (jnp.cos(rotation)[:, None, :], jnp.sin(rotation)[:, None, :])


def rotate(features, cos_table, sin_table):
    half_rot = ROT // 2
    first_half = features[..., :half_rot]
    second = features[..., half_rot:ROT]
    return jnp.concatenate(
        [
            first_half * cos_table - second * sin_table,
            second * cos_table + first_half * sin_table,
            features[..., ROT:],
        ],
        axis=-1,
    )


def unrotate(gradient, cos_table, sin_table):
    half_rot = ROT // 2
    first_half = gradient[..., :half_rot]
    second = gradient[..., half_rot:ROT]
    return jnp.concatenate(
        [
            first_half * cos_table + second * sin_table,
            second * cos_table - first_half * sin_table,
            gradient[..., ROT:],
        ],
        axis=-1,
    )


def adam_update(weight, gradient, moment_one, moment_two, step_rate):
    moment_one = BETA_ONE * moment_one + (1.0 - BETA_ONE) * gradient
    moment_two = BETA_TWO * moment_two + (1.0 - BETA_TWO) * gradient * gradient
    first_hat = moment_one / (1.0 - BETA_ONE**STEP)
    second_hat = moment_two / (1.0 - BETA_TWO**STEP)
    weight = weight - step_rate * (
        first_hat / (jnp.sqrt(second_hat) + ADAM_EPS) + WEIGHT_DECAY * weight
    )
    return (weight, moment_one, moment_two)


def shards(
    block_input,
    out_cotangent,
    token_order,
    seq_lengths,
    w_qkv,
    w_out,
    w_fc1,
    w_fc2,
    vectors,
    mom1_qkv,
    mom1_out,
    mom1_fc1,
    mom1_fc2,
    mom1_vec,
    mom2_qkv,
    mom2_out,
    mom2_fc1,
    mom2_fc2,
    mom2_vec,
):
    tok_rows = block_input.shape[0]
    model_width = block_input.shape[1]
    ctx_count = lax.axis_size("ctx")
    ctx_rank = lax.axis_index("ctx")
    tp_rank = lax.axis_index("tp")
    whole_order = lax.all_gather(token_order, "ctx", axis=1, tiled=True)[0]
    doc_ids, positions = places(whole_order, seq_lengths[0])
    query_doc = lax.dynamic_slice_in_dim(doc_ids, ctx_rank * tok_rows, tok_rows)
    query_pos = lax.dynamic_slice_in_dim(positions, ctx_rank * tok_rows, tok_rows)

    def block_mask(cycle_step):
        anchor = (ctx_rank - cycle_step + ctx_count) % ctx_count
        key_doc = lax.dynamic_slice_in_dim(doc_ids, anchor * tok_rows, tok_rows)
        key_pos = lax.dynamic_slice_in_dim(positions, anchor * tok_rows, tok_rows)
        return (query_doc[:, None] == key_doc[None, :]) & (key_pos[None, :] <= query_pos[:, None])

    lowered = (
        w_qkv.astype(jnp.bfloat16),
        w_out.astype(jnp.bfloat16),
        w_fc1.astype(jnp.bfloat16),
        w_fc2.astype(jnp.bfloat16),
    )
    full_qkv, full_out, full_fc1, full_fc2 = (
        lax.all_gather(lowered[0], ("dp", "ctx"), axis=0, tiled=True),
        lax.all_gather(lowered[1], ("dp", "ctx"), axis=1, tiled=True),
        lax.all_gather(lowered[2], ("dp", "ctx"), axis=0, tiled=True),
        lax.all_gather(lowered[3], ("dp", "ctx"), axis=1, tiled=True),
    )
    head_feat = full_qkv.shape[2]
    heads_local = head_feat // HD
    ff_local = full_fc1.shape[1]
    mat_qkv = full_qkv.reshape(model_width, 3 * head_feat)
    mat_out = full_out[0]
    mat_fc2 = full_fc2[0]
    vec_qkv = lax.dynamic_slice(vectors[0:3], (0, tp_rank * head_feat), (3, head_feat))
    vec_fc1 = lax.dynamic_slice_in_dim(
        vectors[3 : 3 + FF // D].reshape(FF), tp_rank * ff_local, ff_local
    )
    norm_gain = vectors[9]
    norm_shift = vectors[10]
    block_float = block_input.astype(jnp.float32)
    row_mean = jnp.mean(block_float, axis=-1, keepdims=True)
    centered = block_float - row_mean
    inv_std = lax.rsqrt(jnp.mean(centered * centered, axis=-1, keepdims=True) + NORM_EPS)
    normal_x = centered * inv_std
    normed_b = (normal_x * norm_gain + norm_shift).astype(jnp.bfloat16)
    projected = jnp.dot(normed_b, mat_qkv, preferred_element_type=jnp.float32) + vec_qkv.reshape(
        3 * head_feat
    )
    projected = projected.reshape(tok_rows, 3, heads_local, HD)
    cos_table, sin_table = angles(query_pos)
    query = rotate(projected[:, 0], cos_table, sin_table).astype(jnp.bfloat16)
    key_rot = rotate(projected[:, 1], cos_table, sin_table).astype(jnp.bfloat16)
    value = projected[:, 2].astype(jnp.bfloat16)
    own_pair = jnp.stack([key_rot, value])
    key_value = own_pair
    row_top = jnp.full((heads_local, tok_rows), MASKED, jnp.float32)
    row_total = jnp.zeros((heads_local, tok_rows), jnp.float32)
    accumulated = jnp.zeros((heads_local, tok_rows, HD), jnp.float32)
    for cycle_step in range(ctx_count):
        if cycle_step > 0:
            key_value = shifted(key_value, "ctx", 1)
        attn_mask = block_mask(cycle_step)[None]
        scores = (
            jnp.einsum("qhd,khd->hqk", query, key_value[0], preferred_element_type=jnp.float32)
            * SCORE_SCALE
        )
        scores = jnp.where(attn_mask, scores, MASKED)
        new_top = jnp.maximum(row_top, jnp.max(scores, axis=-1))
        attn_probs = jnp.where(attn_mask, jnp.exp(scores - new_top[..., None]), 0.0)
        rescale = jnp.exp(row_top - new_top)
        row_total = row_total * rescale + jnp.sum(attn_probs, axis=-1)
        accumulated = accumulated * rescale[..., None] + jnp.einsum(
            "hqk,khd->hqd",
            attn_probs.astype(jnp.bfloat16),
            key_value[1],
            preferred_element_type=jnp.float32,
        )
        row_top = new_top
    attn_float = accumulated / row_total[..., None]
    log_total = row_top + jnp.log(row_total)
    attended_b = attn_float.transpose(1, 0, 2).reshape(tok_rows, head_feat).astype(jnp.bfloat16)
    hidden = jnp.dot(normed_b, full_fc1, preferred_element_type=jnp.float32) + vec_fc1
    gelu_tanh = partial(jax.nn.gelu, approximate=True)
    active_b = gelu_tanh(hidden).astype(jnp.bfloat16)
    partial_out = jnp.dot(attended_b, mat_out, preferred_element_type=jnp.float32)
    partial_out = partial_out + jnp.dot(active_b, mat_fc2, preferred_element_type=jnp.float32)
    branch = lax.psum(partial_out.astype(jnp.bfloat16), "tp").astype(jnp.float32)
    block_output = (block_float + branch + vectors[7] + vectors[8]).astype(jnp.bfloat16)
    again_input = lax.optimization_barrier((lowered, branch))[0]
    full_qkv, full_out, full_fc1, full_fc2 = (
        lax.all_gather(again_input[0], ("dp", "ctx"), axis=0, tiled=True),
        lax.all_gather(again_input[1], ("dp", "ctx"), axis=1, tiled=True),
        lax.all_gather(again_input[2], ("dp", "ctx"), axis=0, tiled=True),
        lax.all_gather(again_input[3], ("dp", "ctx"), axis=1, tiled=True),
    )
    mat_qkv = full_qkv.reshape(model_width, 3 * head_feat)
    mat_out = full_out[0]
    mat_fc2 = full_fc2[0]
    cot_float = out_cotangent.astype(jnp.float32)
    hidden_back = jnp.einsum(
        "nd,fd->nf", out_cotangent, mat_fc2, preferred_element_type=jnp.float32
    )
    hidden_grad = jax.vjp(gelu_tanh, hidden)[1](hidden_back)[0].astype(jnp.bfloat16)
    grad_fc2 = jnp.einsum("nf,nd->fd", active_b, out_cotangent, preferred_element_type=jnp.float32)
    grad_fc1 = jnp.einsum("nd,nf->df", normed_b, hidden_grad, preferred_element_type=jnp.float32)
    bias_fc1 = jnp.sum(hidden_grad.astype(jnp.float32), axis=0)
    attn_grad = jnp.einsum(
        "nd,fd->nf", out_cotangent, mat_out, preferred_element_type=jnp.float32
    ).astype(jnp.bfloat16)
    grad_out = jnp.einsum(
        "nf,nd->fd", attended_b, out_cotangent, preferred_element_type=jnp.float32
    )
    attn_heads = attn_grad.reshape(tok_rows, heads_local, HD)
    row_delta = jnp.einsum("qhd,hqd->hq", attn_heads.astype(jnp.float32), attn_float)
    key_value = own_pair
    kv_grads = jnp.zeros((2, tok_rows, heads_local, HD), jnp.float32)
    query_grad = jnp.zeros((tok_rows, heads_local, HD), jnp.float32)
    for cycle_step in range(ctx_count):
        if cycle_step > 0:
            key_value = shifted(key_value, "ctx", 1)
        attn_mask = block_mask(cycle_step)[None]
        scores = (
            jnp.einsum("qhd,khd->hqk", query, key_value[0], preferred_element_type=jnp.float32)
            * SCORE_SCALE
        )
        attn_probs = jnp.where(attn_mask, jnp.exp(scores - log_total[..., None]), 0.0)
        probs_b = attn_probs.astype(jnp.bfloat16)
        prob_grad = jnp.einsum(
            "qhd,khd->hqk", attn_heads, key_value[1], preferred_element_type=jnp.float32
        )
        score_grad = (attn_probs * (prob_grad - row_delta[..., None])).astype(jnp.bfloat16)
        query_grad = (
            query_grad
            + jnp.einsum(
                "hqk,khd->qhd", score_grad, key_value[0], preferred_element_type=jnp.float32
            )
            * SCORE_SCALE
        )
        key_part = (
            jnp.einsum("hqk,qhd->khd", score_grad, query, preferred_element_type=jnp.float32)
            * SCORE_SCALE
        )
        value_part = jnp.einsum(
            "hqk,qhd->khd", probs_b, attn_heads, preferred_element_type=jnp.float32
        )
        kv_grads = kv_grads + jnp.stack([key_part, value_part])
        kv_grads = shifted(kv_grads.astype(jnp.bfloat16), "ctx", 1).astype(kv_grads.dtype)
    pre_grad = (
        jnp.stack(
            [
                unrotate(query_grad, cos_table, sin_table),
                unrotate(kv_grads[0], cos_table, sin_table),
                kv_grads[1],
            ],
            axis=1,
        )
        .reshape(tok_rows, 3 * head_feat)
        .astype(jnp.bfloat16)
    )
    grad_qkv = jnp.einsum("nd,nf->df", normed_b, pre_grad, preferred_element_type=jnp.float32)
    bias_qkv = jnp.sum(pre_grad.astype(jnp.float32), axis=0).reshape(3, head_feat)
    normed_part = jnp.einsum("nf,df->nd", pre_grad, mat_qkv, preferred_element_type=jnp.float32)
    normed_part = normed_part + jnp.einsum(
        "nf,df->nd", hidden_grad, full_fc1, preferred_element_type=jnp.float32
    )
    normed_grad = lax.psum(normed_part.astype(jnp.bfloat16), "tp").astype(jnp.float32)
    scaled_grad = normed_grad * norm_gain
    input_grad = cot_float + inv_std * (
        scaled_grad
        - jnp.mean(scaled_grad, axis=-1, keepdims=True)
        - normal_x * jnp.mean(scaled_grad * normal_x, axis=-1, keepdims=True)
    )
    gain_grad = jnp.sum(normed_grad * normal_x, axis=0)
    shift_grad = jnp.sum(normed_grad, axis=0)
    cot_sum = jnp.sum(cot_float, axis=0)
    first_rank = (tp_rank == 0).astype(jnp.float32)
    qkv_rows = lax.dynamic_update_slice(
        jnp.zeros((3, model_width), jnp.float32), bias_qkv, (0, tp_rank * head_feat)
    )
    fc1_rows = lax.dynamic_update_slice_in_dim(
        jnp.zeros((FF,), jnp.float32), bias_fc1, tp_rank * ff_local, 0
    )
    common_rows = jnp.stack([cot_sum, cot_sum, gain_grad, shift_grad]) * first_rank
    vector_term = jnp.concatenate(
        [qkv_rows, fc1_rows.reshape(FF // D, model_width), common_rows], axis=0
    )
    term_qkv = grad_qkv.reshape(model_width, 3, head_feat)
    term_out = grad_out[None]
    term_fc2 = grad_fc2[None]
    sum_qkv, sum_out, sum_fc1, sum_fc2 = (
        lax.psum_scatter(term_qkv, ("dp", "ctx"), scatter_dimension=0, tiled=True),
        lax.psum_scatter(term_out, ("dp", "ctx"), scatter_dimension=1, tiled=True),
        lax.psum_scatter(grad_fc1, ("dp", "ctx"), scatter_dimension=0, tiled=True),
        lax.psum_scatter(term_fc2, ("dp", "ctx"), scatter_dimension=1, tiled=True),
    )
    vector_grad = lax.psum(vector_term, ("dp", "ctx", "tp"))
    new_qkv = adam_update(w_qkv, sum_qkv, mom1_qkv, mom2_qkv, 2.0 / math.sqrt(D))
    new_out = adam_update(w_out, sum_out, mom1_out, mom2_out, 16.0 / math.sqrt(D))
    new_fc1 = adam_update(w_fc1, sum_fc1, mom1_fc1, mom2_fc1, 2.0 / math.sqrt(D))
    new_fc2 = adam_update(w_fc2, sum_fc2, mom1_fc2, mom2_fc2, 2.0 / math.sqrt(FF))
    new_vec = adam_update(vectors, vector_grad, mom1_vec, mom2_vec, 0.2)
    return (
        block_output,
        input_grad,
        new_qkv[0],
        new_out[0],
        new_fc1[0],
        new_fc2[0],
        new_vec[0],
        new_qkv[1],
        new_out[1],
        new_fc1[1],
        new_fc2[1],
        new_vec[1],
        new_qkv[2],
        new_out[2],
        new_fc1[2],
        new_fc2[2],
        new_vec[2],
    )


def solution(mesh):
    in_specs = (
        P(("dp", "ctx"), None),
        P(("dp", "ctx"), None),
        P("dp", "ctx"),
        P("dp", None),
        P(("dp", "ctx"), None, "tp"),
        P("tp", ("dp", "ctx"), None),
        P(("dp", "ctx"), "tp"),
        P("tp", ("dp", "ctx"), None),
        P(),
        P(("dp", "ctx"), None, "tp"),
        P("tp", ("dp", "ctx"), None),
        P(("dp", "ctx"), "tp"),
        P("tp", ("dp", "ctx"), None),
        P(),
        P(("dp", "ctx"), None, "tp"),
        P("tp", ("dp", "ctx"), None),
        P(("dp", "ctx"), "tp"),
        P("tp", ("dp", "ctx"), None),
        P(),
    )
    out_specs = (
        P(("dp", "ctx"), None),
        P(("dp", "ctx"), None),
        P(("dp", "ctx"), None, "tp"),
        P("tp", ("dp", "ctx"), None),
        P(("dp", "ctx"), "tp"),
        P("tp", ("dp", "ctx"), None),
        P(),
        P(("dp", "ctx"), None, "tp"),
        P("tp", ("dp", "ctx"), None),
        P(("dp", "ctx"), "tp"),
        P("tp", ("dp", "ctx"), None),
        P(),
        P(("dp", "ctx"), None, "tp"),
        P("tp", ("dp", "ctx"), None),
        P(("dp", "ctx"), "tp"),
        P("tp", ("dp", "ctx"), None),
        P(),
    )
    return jax.shard_map(shards, mesh=mesh, in_specs=in_specs, out_specs=out_specs, check_vma=False)
```

profile of v0, /device:TPU:1, one launch (start us, length us, event | category | flops | bytes accessed | tf_op | source)
XLA Modules:
  0.0 5677.3 jit_solution(10051673609171297651)
XLA Ops:
  11.3 21.1 all_gather.27
  34.1 302.1 %all-gather.9.cloned.1.call-done = bf16[2048,3,1024]{2,0,1:T(8,128)(2,1)} async-done(((bf16[32,3,1024]{2,0,1:T(8,128)(2,1)}), bf16[2048,3,1024]{2,0,1:T(8,128)(2,1)}) %all-gather.9.cloned.1.call-update) | async-done | bytes 12582928 | tf_op jit(solution)/shard_map/all_gather | solution.py:131
  336.2 16.8 copy.167
  365.4 12.0 collective-permute-done
  390.5 14.9 collective-permute-done.2
  406.6 14.4 collective-permute-done.3
  425.3 14.9 collective-permute-done.4
  444.6 23.6 collective-permute-done.5
  476.1 21.6 collective-permute-done.6
  511.6 305.9 %all-gather.13.cloned.1.call-done = bf16[2048,4096]{1,0:T(8,128)(2,1)} async-done(((bf16[32,4096]{1,0:T(8,128)(2,1)}), bf16[2048,4096]{1,0:T(8,128)(2,1)}) %all-gather.13.cloned.1.call-update) | async-done | bytes 16777232 | tf_op jit(solution)/shard_map/all_gather | solution.py:133
  827.1 13.2 convolution_bitcast_fusion
  840.3 324.5 %reduce-scatter.7.cloned.1.call-done = f32[1,16,2048]{2,1,0:T(8,128)} async-done(((f32[1,1024,2048]{2,1,0:T(8,128)}), f32[1,16,2048]{2,1,0:T(8,128)}) %reduce-scatter.7.cloned.1.call-update) | async-done | bytes 131088 | tf_op jit(solution)/shard_map/reduce_scatter | solution.py:300
  1166.8 769.3 %reduce-scatter.11.cloned.1.call-done = f32[1,64,2048]{2,1,0:T(8,128)} async-done(((f32[1,4096,2048]{2,1,0:T(8,128)}), f32[1,64,2048]{2,1,0:T(8,128)}) %reduce-scatter.11.cloned.1.call-update) | async-done | bytes 524304 | tf_op jit(solution)/shard_map/reduce_scatter | solution.py:302
  1943.9 288.4 %all-gather.17.cloned.1.call-done = bf16[1,1024,2048]{2,1,0:T(8,128)(2,1)} async-done(((bf16[1,16,2048]{2,1,0:T(8,128)(2,1)}), bf16[1,1024,2048]{2,1,0:T(8,128)(2,1)}) %all-gather.17.cloned.1.call-update) | async-done | bytes 4194320 | tf_op jit(solution)/shard_map/all_gather | solution.py:200
  2293.8 16.3 collective-permute-done.11
  2310.9 18.4 collective-permute-done.12
  2333.6 16.6 collective-permute-done.13
  2352.8 18.4 collective-permute-done.14
  2372.1 303.7 %all-gather.19.cloned.1.call-done = bf16[2048,3,1024]{2,0,1:T(8,128)(2,1)} async-done(((bf16[32,3,1024]{2,0,1:T(8,128)(2,1)}), bf16[2048,3,1024]{2,0,1:T(8,128)(2,1)}) %all-gather.19.cloned.1.call-update) | async-done | bytes 12582928 | tf_op jit(solution)/shard_map/all_gather | solution.py:199
  2675.8 17.3 copy.209
  2693.2 377.1 %all-gather.21.cloned.1.call-done = bf16[1,4096,2048]{2,1,0:T(8,128)(2,1)} async-done(((bf16[1,64,2048]{2,1,0:T(8,128)(2,1)}), bf16[1,4096,2048]{2,1,0:T(8,128)(2,1)}) %all-gather.21.cloned.1.call-update) | async-done | bytes 16777232 | tf_op jit(solution)/shard_map/all_gather | solution.py:202
  3070.3 13.2 convert_reduce_fusion
  3083.5 379.6 %all-gather.23.cloned.1.call-done = bf16[2048,4096]{1,0:T(8,128)(2,1)} async-done(((bf16[32,4096]{1,0:T(8,128)(2,1)}), bf16[2048,4096]{1,0:T(8,128)(2,1)}) %all-gather.23.cloned.1.call-update) | async-done | bytes 16777232 | tf_op jit(solution)/shard_map/all_gather | solution.py:201
  3463.0 12.7 fusion.263
  3483.2 370.9 %all-gather.15.cloned.1.call-done = bf16[1,4096,2048]{2,1,0:T(8,128)(2,1)} async-done(((bf16[1,64,2048]{2,1,0:T(8,128)(2,1)}), bf16[1,4096,2048]{2,1,0:T(8,128)(2,1)}) %all-gather.15.cloned.1.call-update) | async-done | bytes 16777232 | tf_op jit(solution)/shard_map/all_gather | solution.py:134
  3863.7 315.7 %all-gather.11.cloned.1.call-done = bf16[1,1024,2048]{2,1,0:T(8,128)(2,1)} async-done(((bf16[1,16,2048]{2,1,0:T(8,128)(2,1)}), bf16[1,1024,2048]{2,1,0:T(8,128)(2,1)}) %all-gather.11.cloned.1.call-update) | async-done | bytes 4194320 | tf_op jit(solution)/shard_map/all_gather | solution.py:132
  4184.0 66.9 %all-reduce.6.cloned.1.call-done = (bf16[128,2048]{1,0:T(8,128)(2,1)}, bf16[128,2048]{1,0:T(8,128)(2,1)}) async-done(((bf16[128,2048]{1,0:T(8,128)(2,1)}, bf16[128,2048]{1,0:T(8,128)(2,1)}), (bf16[128,2048]{1,0:T(8,128)(2,1)}, bf16[128,2048]{1,0:T(8,128)(2,1)})) %all-reduce.6.cloned.1.call-update) | async-done | bytes 1048592 | tf_op jit(solution)/shard_map/psum | solution.py:195
  4256.4 12.0 fusion.132
  4269.6 13.3 fusion.246
  4283.0 114.8 %all-reduce.4.cloned.1.call-done = f32[11,2048]{1,0:T(8,128)} async-done(((f32[11,2048]{1,0:T(8,128)}), f32[11,2048]{1,0:T(8,128)}) %all-reduce.4.cloned.1.call-update) | async-done | bytes 90128 | tf_op jit(solution)/shard_map/psum | solution.py:304
  4399.6 544.6 %reduce-scatter.5.cloned.1.call-done = f32[32,3,1024]{2,0,1:T(8,128)} async-done(((f32[2048,3,1024]{2,0,1:T(8,128)}), f32[32,3,1024]{2,0,1:T(8,128)}) %reduce-scatter.5.cloned.1.call-update) | async-done | bytes 393232 | tf_op jit(solution)/shard_map/reduce_scatter | solution.py:299
  4946.4 721.7 %reduce-scatter.9.cloned.1.call-done = f32[32,4096]{1,0:T(8,128)} async-done(((f32[2048,4096]{1,0:T(8,128)}), f32[32,4096]{1,0:T(8,128)}) %reduce-scatter.9.cloned.1.call-update) | async-done | bytes 524304 | tf_op jit(solution)/shard_map/reduce_scatter | solution.py:301
  (372 shorter events, 185.5 us)
Async XLA Ops:
  7.2 328.9 %all-gather.9.cloned.1.call-start = ((), (), s32[]{:S(2)}) async-start(), calls=%async_computation.4 | async-start | bytes 12779520 | tf_op jit(solution)/shard_map/all_gather | solution.py:131
  9.1 808.3 %all-gather.13.cloned.1.call-start = ((), (), s32[]{:S(2)}) async-start(), calls=%async_computation.6 | async-start | bytes 17039360 | tf_op jit(solution)/shard_map/all_gather | solution.py:133
  11.0 1153.8 %reduce-scatter.7.cloned.1.call-start = ((), (), s32[]{:S(2)}) async-start(), calls=%async_computation.13 | async-start | bytes 8519680 | tf_op jit(solution)/shard_map/reduce_scatter | solution.py:300
  365.3 12.1 collective-permute-start
  377.4 11.6 collective-permute-start.1
  389.0 16.4 collective-permute-start.2
  405.4 15.5 collective-permute-start.3
  421.0 19.3 collective-permute-start.4
  440.2 28.0 collective-permute-start.5
  468.2 29.4 collective-permute-start.6
  508.7 1427.4 %reduce-scatter.11.cloned.1.call-start = ((), (), s32[]{:S(2)}) async-start(), calls=%async_computation.15 | async-start | bytes 34078720 | tf_op jit(solution)/shard_map/reduce_scatter | solution.py:302
  840.3 1392.0 %all-gather.17.cloned.1.call-start = ((), (), s32[]{:S(2)}) async-start(), calls=%async_computation.8 | async-start | bytes 4259840 | tf_op jit(solution)/shard_map/all_gather | solution.py:200
  1939.3 736.5 %all-gather.19.cloned.1.call-start = ((), (), s32[]{:S(2)}) async-start(), calls=%async_computation.9 | async-start | bytes 12779520 | tf_op jit(solution)/shard_map/all_gather | solution.py:199
  1939.9 1130.4 %all-gather.21.cloned.1.call-start = ((), (), s32[]{:S(2)}) async-start(), calls=%async_computation.10 | async-start | bytes 17039360 | tf_op jit(solution)/shard_map/all_gather | solution.py:202
  1940.6 1522.4 %all-gather.23.cloned.1.call-start = ((), (), s32[]{:S(2)}) async-start(), calls=%async_computation.11 | async-start | bytes 17039360 | tf_op jit(solution)/shard_map/all_gather | solution.py:201
  1941.4 1912.7 %all-gather.15.cloned.1.call-start = ((), (), s32[]{:S(2)}) async-start(), calls=%async_computation.7 | async-start | bytes 17039360 | tf_op jit(solution)/shard_map/all_gather | solution.py:134
  1942.1 2237.2 %all-gather.11.cloned.1.call-start = ((), (), s32[]{:S(2)}) async-start(), calls=%async_computation.5 | async-start | bytes 4259840 | tf_op jit(solution)/shard_map/all_gather | solution.py:132
  1943.7 2307.2 %all-reduce.6.cloned.1.call-start = ((), (), s32[]{:S(2)}) async-start(), calls=%async_computation.17 | async-start | bytes 2097152 | tf_op jit(solution)/shard_map/psum | solution.py:195
  2243.2 12.6 collective-permute-start.7
  2256.0 12.5 collective-permute-start.8
  2268.6 11.8 collective-permute-start.9
  2280.6 11.8 collective-permute-start.10
  2292.5 17.5 collective-permute-start.11
  2310.3 19.1 collective-permute-start.12
  2329.5 20.7 collective-permute-start.13
  2350.3 20.8 collective-permute-start.14
  4183.5 214.4 %all-reduce.4.cloned.1.call-start = ((), (), s32[]{:S(2)}) async-start(), calls=%async_computation.16 | async-start | bytes 262144 | tf_op jit(solution)/shard_map/psum | solution.py:304
  4256.4 687.8 %reduce-scatter.5.cloned.1.call-start = ((), (), s32[]{:S(2)}) async-start(), calls=%async_computation.12 | async-start | bytes 25559040 | tf_op jit(solution)/shard_map/reduce_scatter | solution.py:299
  4268.4 1399.7 %reduce-scatter.9.cloned.1.call-start = ((), (), s32[]{:S(2)}) async-start(), calls=%async_computation.14 | async-start | bytes 34078720 | tf_op jit(solution)/shard_map/reduce_scatter | solution.py:301
  4283.0 1385.1 %copy-start.29 = (f32[32,4096]{1,0:T(8,128)S(1)}, f32[32,4096]{1,0:T(8,128)}, u32[]{:S(2)}) copy-start(f32[32,4096]{1,0:T(8,128)} %param.25) | copy-start | bytes 1572868
  4283.0 1385.1 %copy-start.33 = (f32[32,4096]{1,0:T(8,128)S(1)}, f32[32,4096]{1,0:T(8,128)}, u32[]{:S(2)}) copy-start(f32[32,4096]{1,0:T(8,128)} %param.30) | copy-start | bytes 1572868
  4283.0 1385.1 %copy-start.34 = (f32[32,4096]{1,0:T(8,128)S(1)}, f32[32,4096]{1,0:T(8,128)}, u32[]{:S(2)}) copy-start(f32[32,4096]{1,0:T(8,128)} %param.35) | copy-start | bytes 1572868
  (94 other events, 7905.5 us)
Sparse Core Ops, SparseCore 0:
  9.7 326.3 all-gather.8
  338.4 479.0 all-gather.12
  819.8 344.9 reduce-scatter.6
  1167.1 769.0 reduce-scatter.10
  1939.4 292.8 all-gather.16
  2233.8 441.9 all-gather.18
  2678.0 392.2 all-gather.20
  3072.5 390.5 all-gather.22
  3465.3 388.7 all-gather.14
  3856.2 323.1 all-gather.10
  4183.6 67.3 all-reduce.5
  4256.8 140.9 all-reduce.3
  4400.3 543.8 reduce-scatter.4
  4946.5 721.6 reduce-scatter.8
where the time goes:
time: 5690 us; the launch traced here: 5680 us
  waiting for transfers between devices  5410 us (95%)
  matrix products  133 us (2%)
    reduce_scatter x1, waiting for transfers between devices, shards(): lax.psum_scatter(term_fc2, ('dp', 'ctx'), scatter_dimension=1, tiled=True)  769 us
    reduce_scatter x1, waiting for transfers between devices, shards(): lax.psum_scatter(grad_fc1, ('dp', 'ctx'), scatter_dimension=0, tiled=True)  722 us
    reduce_scatter x1, waiting for transfers between devices, shards(): lax.psum_scatter(term_qkv, ('dp', 'ctx'), scatter_dimension=0, tiled=True)  545 us
    all_gather x1, waiting for transfers between devices, shards(): lax.all_gather(again_input[2], ('dp', 'ctx'), axis=0, tiled=True)  380 us
    all_gather x1, waiting for transfers between devices, shards(): lax.all_gather(again_input[3], ('dp', 'ctx'), axis=1, tiled=True)  377 us
    all_gather x1, waiting for transfers between devices, shards(): lax.all_gather(lowered[3], ('dp', 'ctx'), axis=1, tiled=True)  371 us
    reduce_scatter x1, waiting for transfers between devices, shards(): lax.psum_scatter(term_out, ('dp', 'ctx'), scatter_dimension=1, tiled=True)  324 us
    all_gather x1, waiting for transfers between devices, shards(): lax.all_gather(lowered[1], ('dp', 'ctx'), axis=1, tiled=True)  316 us
  transfers between devices with their start and end apart: 29, of which 29 were waited for; matrix products, arithmetic and copies ran while one was open for 3% of the time, Pallas kernels for 0%

commit v1 on v0

v1 whole, which is shorter than its diff:
```python
import math

import jax
import jax.numpy as jnp
from jax import lax
from jax.experimental import pallas as pl
from jax.experimental.pallas import tpu as pltpu
from jax.sharding import PartitionSpec as P

D = 2048
FF = 8192
HD = 64
ROT = 32
STEP = 10

NORM_EPS = 1e-05
SCORE_SCALE = 0.125
MASKED = -1e30
ROPE_BASE = 10000.0
BETA_ONE = 0.9
BETA_TWO = 0.95
ADAM_EPS = 1e-08
WEIGHT_DECAY = 0.1

N_DP = 8
N_CTX = 8
N_TP = 2
TEAM = N_CTX * N_TP
GROUP = 1024
HALF_ROWS = 64
FEAT = D // TEAM
HIDDEN = FF // TEAM
QKV = 3 * FEAT
Q_BLOCK = 256

BF = jnp.bfloat16
F32 = jnp.float32


def adam_update(weight, gradient, moment_one, moment_two, step_rate):
    moment_one = BETA_ONE * moment_one + (1.0 - BETA_ONE) * gradient
    moment_two = BETA_TWO * moment_two + (1.0 - BETA_TWO) * gradient * gradient
    first_hat = moment_one / (1.0 - BETA_ONE**STEP)
    second_hat = moment_two / (1.0 - BETA_TWO**STEP)
    weight = weight - step_rate * (
        first_hat / (jnp.sqrt(second_hat) + ADAM_EPS) + WEIGHT_DECAY * weight
    )
    return (weight, moment_one, moment_two)


def gelu_and_slope(hidden):
    root = math.sqrt(2.0 / math.pi)
    square = hidden * hidden
    bent = jnp.tanh(root * (hidden + 0.044715 * hidden * square))
    value = 0.5 * hidden * (1.0 + bent)
    slope = 0.5 * (1.0 + bent) + 0.5 * hidden * (1.0 - bent * bent) * root * (
        1.0 + 3.0 * 0.044715 * square
    )
    return (value, slope)


def dot(left, right, dims):
    return lax.dot_general(left, right, (dims, ((), ())), preferred_element_type=F32)


def attention_kernel(
    pre_ref,
    dattn_ref,
    cos_ref,
    sin_ref,
    tok_ref,
    start_ref,
    key_tok_ref,
    attended_ref,
    dpre_ref,
    sums_ref,
    key_scr,
    value_scr,
    dkey_scr,
    dvalue_scr,
):
    step = pl.program_id(0)
    lane = lax.broadcasted_iota(jnp.int32, (1, FEAT), 1)
    early = (lane % HD) < (ROT // 2)
    first_head = lane < HD

    def partner(value):
        return jnp.where(
            early,
            pltpu.roll(value, FEAT - ROT // 2, axis=1),
            pltpu.roll(value, ROT // 2, axis=1),
        )

    @pl.when(step == 0)
    def _():
        key = pre_ref[:, FEAT : 2 * FEAT]
        key_scr[...] = (key * cos_ref[...] + partner(key) * sin_ref[...]).astype(BF)
        value_scr[...] = pre_ref[:, 2 * FEAT :].astype(BF)
        dkey_scr[...] = jnp.zeros_like(dkey_scr)
        dvalue_scr[...] = jnp.zeros_like(dvalue_scr)
        sums_ref[...] = jnp.zeros_like(sums_ref)

    rows = pl.ds(step * Q_BLOCK, Q_BLOCK)
    cos_rows = cos_ref[rows, :]
    sin_rows = sin_ref[rows, :]
    query = pre_ref[rows, :FEAT]
    query = (query * cos_rows + partner(query) * sin_rows).astype(BF) * jnp.asarray(SCORE_SCALE, BF)
    dattn = dattn_ref[rows, :]
    key = key_scr[...]
    value = value_scr[...]
    tok = tok_ref[rows, :]
    start = start_ref[rows, :]
    key_tok = key_tok_ref[...]
    mask = (key_tok <= tok) & (key_tok >= start)
    zero = jnp.zeros((), BF)
    out_parts = []
    dquery_parts = []
    for head in range(2):
        inside = first_head if head == 0 else jnp.logical_not(first_head)
        query_h = jnp.where(inside, query, zero)
        dattn_h = jnp.where(inside, dattn, zero)
        scores = dot(query_h, key, ((1,), (1,)))
        scores = jnp.where(mask, scores, MASKED)
        top = jnp.max(scores, axis=1, keepdims=True)
        probs = jnp.exp(scores - top)
        probs = probs * (1.0 / jnp.sum(probs, axis=1, keepdims=True))
        probs_b = probs.astype(BF)
        out = dot(probs_b, value, ((1,), (0,)))
        delta = jnp.sum(
            jnp.where(inside, out, 0.0) * dattn_h.astype(F32), axis=1, keepdims=True
        )
        dprobs = dot(dattn_h, value, ((1,), (1,)))
        dscore = (probs * (dprobs - delta)).astype(BF)
        dquery_parts.append(dot(dscore, key, ((1,), (0,))))
        dkey_scr[...] += dot(dscore, query_h, ((0,), (0,)))
        dvalue_scr[...] += dot(probs_b, dattn_h, ((0,), (0,)))
        out_parts.append(out)
    attended_ref[rows, :] = jnp.where(first_head, out_parts[0], out_parts[1]).astype(BF)
    dquery = jnp.where(first_head, dquery_parts[0], dquery_parts[1]) * SCORE_SCALE
    dquery = (dquery * cos_rows - partner(dquery) * sin_rows).astype(BF)
    dpre_ref[rows, :FEAT] = dquery
    sums_ref[0:1, :FEAT] += jnp.sum(dquery.astype(F32), axis=0, keepdims=True)

    @pl.when(step == pl.num_programs(0) - 1)
    def _():
        dkey = dkey_scr[...]
        dkey = (dkey * cos_ref[...] - partner(dkey) * sin_ref[...]).astype(BF)
        dvalue = dvalue_scr[...].astype(BF)
        dpre_ref[:, FEAT : 2 * FEAT] = dkey
        dpre_ref[:, 2 * FEAT :] = dvalue
        sums_ref[0:1, FEAT : 2 * FEAT] = jnp.sum(dkey.astype(F32), axis=0, keepdims=True)
        sums_ref[0:1, 2 * FEAT :] = jnp.sum(dvalue.astype(F32), axis=0, keepdims=True)


def attention(pre, dattn, cos_table, sin_table, tok, start):
    tokens = pre.shape[0]
    whole = pl.BlockSpec(memory_space=pltpu.VMEM)
    return pl.pallas_call(
        attention_kernel,
        grid=(tokens // Q_BLOCK,),
        out_shape=(
            jax.ShapeDtypeStruct((tokens, FEAT), BF),
            jax.ShapeDtypeStruct((tokens, QKV), BF),
            jax.ShapeDtypeStruct((8, QKV), F32),
        ),
        in_specs=[whole] * 7,
        out_specs=(whole, whole, whole),
        scratch_shapes=[
            pltpu.VMEM((tokens, FEAT), BF),
            pltpu.VMEM((tokens, FEAT), BF),
            pltpu.VMEM((tokens, FEAT), F32),
            pltpu.VMEM((tokens, FEAT), F32),
        ],
        compiler_params=pltpu.CompilerParams(vmem_limit_bytes=40 * 2**20),
        cost_estimate=pl.CostEstimate(
            flops=7 * 2 * 2 * tokens * tokens * HD,
            bytes_accessed=8 * 2**20,
            transcendentals=2 * tokens * tokens,
        ),
    )(pre, dattn, cos_table, sin_table, tok[:, None], start[:, None], tok[None, :])


def swap(value):
    return lax.ppermute(value, "tp", [(0, 1), (1, 0)])


def spread(value, axis, count):
    return lax.all_to_all(
        jnp.broadcast_to(value[None], (count,) + value.shape), axis, 0, 0, tiled=True
    )


def transposed(value):
    pairs = [(a * N_CTX + b, b * N_CTX + a) for a in range(N_DP) for b in range(N_CTX)]
    return lax.ppermute(value, ("dp", "ctx"), pairs)


def shards(
    block_input,
    out_cotangent,
    token_order,
    seq_lengths,
    w_qkv,
    w_out,
    w_fc1,
    w_fc2,
    vectors,
    mom1_qkv,
    mom1_out,
    mom1_fc1,
    mom1_fc2,
    mom1_vec,
    mom2_qkv,
    mom2_out,
    mom2_fc1,
    mom2_fc2,
    mom2_vec,
):
    ctx_rank = lax.axis_index("ctx")
    tp_rank = lax.axis_index("tp")
    team_rank = ctx_rank * N_TP + tp_rank
    own_d = D // (N_DP * N_CTX)
    out_rows = w_out.shape[1]
    fc2_rows = w_fc2.shape[1]

    columns = jnp.concatenate(
        [w_qkv[:, part].reshape(own_d, N_CTX, FEAT) for part in range(3)]
        + [w_fc1.reshape(own_d, N_CTX, HIDDEN)],
        axis=2,
    ).astype(BF)
    columns = lax.all_to_all(columns.transpose(1, 0, 2), "ctx", 0, 0, tiled=True)
    columns = columns.reshape(N_CTX * own_d, QKV + HIDDEN)
    w_in = lax.all_gather(columns, "dp", axis=0, tiled=True)
    rows = transposed(jnp.concatenate([w_out[0], w_fc2[0]], axis=0).astype(BF))
    rows = lax.all_gather(rows, "dp", axis=0, tiled=False)
    w_back = jnp.concatenate(
        [rows[:, :out_rows].reshape(FEAT, D), rows[:, out_rows:].reshape(HIDDEN, D)], axis=0
    )

    def half(value, axis=0):
        return lax.dynamic_slice_in_dim(value, tp_rank * HALF_ROWS, HALF_ROWS, axis)

    x_own = half(block_input).astype(F32)
    dy_own = half(out_cotangent)
    tok_own = half(token_order[0])
    row_mean = jnp.mean(x_own, axis=-1, keepdims=True)
    centered = x_own - row_mean
    inv_std = lax.rsqrt(jnp.mean(centered * centered, axis=-1, keepdims=True) + NORM_EPS)
    normal_x = centered * inv_std
    norm_gain = vectors[9]
    norm_shift = vectors[10]
    normed_own = (normal_x * norm_gain + norm_shift).astype(BF)

    def whole_group(value):
        mine = spread(value, "ctx", N_CTX)
        mine = mine.reshape((N_CTX * HALF_ROWS,) + value.shape[1:])
        return jnp.concatenate([mine, swap(mine)], axis=0)

    normed = whole_group(normed_own)
    tok = whole_group(tok_own)
    dy = whole_group(dy_own)

    ends = jnp.cumsum(seq_lengths[0])
    starts = ends - seq_lengths[0]
    inside = (tok[:, None] >= starts[None, :]) & (tok[:, None] < ends[None, :])
    first = jnp.sum(jnp.where(inside, starts[None, :], 0), axis=1)
    position = (tok - first).astype(F32)
    lane = jnp.arange(FEAT) % HD
    inverse = ROPE_BASE ** (-(2.0 * (lane % (ROT // 2)).astype(F32)) / ROT)
    inverse = jnp.where(lane < ROT, inverse, 0.0)
    rotation = position[:, None] * inverse[None, :]
    cos_table = jnp.cos(rotation)
    sin_table = jnp.sin(rotation) * jnp.where(lane < ROT // 2, -1.0, 1.0)

    bias_qkv = lax.dynamic_slice(vectors, (0, tp_rank * (D // N_TP) + ctx_rank * FEAT), (3, FEAT))
    bias_fc1 = lax.dynamic_slice_in_dim(
        vectors[3:7].reshape(FF), tp_rank * (FF // N_TP) + ctx_rank * HIDDEN, HIDDEN
    )
    pre = dot(normed, w_in, ((1,), (0,)))
    back = dot(dy, w_back, ((1,), (1,)))
    hidden = pre[:, QKV:] + bias_fc1
    pre_qkv = pre[:, :QKV] + bias_qkv.reshape(QKV)
    active, slope = gelu_and_slope(hidden)
    active = active.astype(BF)
    dhid = (back[:, FEAT:] * slope).astype(BF)
    dattn = back[:, :FEAT].astype(BF)
    attended, dpre, dpre_sums = attention(pre_qkv, dattn, cos_table, sin_table, tok, first)

    grad_fc1 = dot(normed, dhid, ((0,), (0,))).astype(BF)
    grad_fc1 = lax.psum_scatter(grad_fc1, "dp", scatter_dimension=0, tiled=True)
    grad_fc2 = dot(active, dy, ((0,), (0,))).astype(BF)
    grad_fc2 = lax.psum_scatter(grad_fc2, "dp", scatter_dimension=0, tiled=True)
    grad_out = dot(attended, dy, ((0,), (0,))).astype(BF)
    grad_qkv = dot(normed, dpre, ((0,), (0,))).astype(BF)

    def summed(value):
        pieces = value.reshape((N_DP, value.shape[0] // N_DP) + value.shape[1:])
        pieces = lax.all_to_all(pieces, "dp", 0, 0, tiled=True)
        return jnp.sum(pieces.astype(F32), axis=0)

    grad_qkv = summed(grad_qkv).astype(BF)
    grad_out = summed(grad_out).astype(BF)
    back_rows = transposed(jnp.concatenate([grad_out, grad_fc2], axis=0)).astype(F32)
    sum_out = back_rows[None, :out_rows]
    sum_fc2 = back_rows[None, out_rows:]
    back_columns = jnp.concatenate([grad_qkv, grad_fc1], axis=1)
    back_columns = back_columns.reshape(N_CTX, own_d, QKV + HIDDEN)
    back_columns = lax.all_to_all(back_columns, "ctx", 0, 0, tiled=True).astype(F32)
    sum_qkv = jnp.stack(
        [
            back_columns[:, :, part * FEAT : (part + 1) * FEAT]
            .transpose(1, 0, 2)
            .reshape(own_d, N_CTX * FEAT)
            for part in range(3)
        ],
        axis=1,
    )
    sum_fc1 = back_columns[:, :, QKV:].transpose(1, 0, 2).reshape(own_d, N_CTX * HIDDEN)

    def to_owner(left, right, dims):
        rows_half = N_CTX * HALF_ROWS
        theirs = dot(left[rows_half:], right, dims).astype(BF)
        mine = dot(left[:rows_half], right, dims)
        mine = (mine + swap(theirs).astype(F32)).astype(BF)
        mine = mine.reshape(N_CTX, HALF_ROWS, D)
        return jnp.sum(lax.all_to_all(mine, "ctx", 0, 0, tiled=True).astype(F32), axis=0)

    def both_halves(value):
        other = swap(value)
        first_core = tp_rank == 0
        return jnp.concatenate(
            [jnp.where(first_core, value, other), jnp.where(first_core, other, value)], axis=0
        )

    branch = to_owner(jnp.concatenate([attended, active], axis=1), w_back, ((1,), (0,)))
    block_output = both_halves((x_own + branch + vectors[7] + vectors[8]).astype(BF))
    normed_grad = to_owner(jnp.concatenate([dpre, dhid], axis=1), w_in, ((1,), (1,)))
    scaled_grad = normed_grad * norm_gain
    input_grad = dy_own.astype(F32) + inv_std * (
        scaled_grad
        - jnp.mean(scaled_grad, axis=-1, keepdims=True)
        - normal_x * jnp.mean(scaled_grad * normal_x, axis=-1, keepdims=True)
    )
    input_grad = both_halves(input_grad)

    dy_sum = jnp.sum(dy.astype(F32), axis=0)
    dy_sum = lax.dynamic_slice_in_dim(dy_sum, team_rank * FEAT, FEAT)
    norm_terms = jnp.stack([jnp.sum(normed_grad * normal_x, axis=0), jnp.sum(normed_grad, axis=0)])
    norm_terms = norm_terms.reshape(2, TEAM, FEAT).transpose(1, 0, 2)
    norm_terms = jnp.sum(lax.all_to_all(norm_terms, ("ctx", "tp"), 0, 0, tiled=True), axis=0)
    terms = jnp.concatenate(
        [
            dpre_sums[0],
            jnp.sum(dhid.astype(F32), axis=0),
            dy_sum,
            norm_terms.reshape(2 * FEAT),
        ]
    )
    terms = jnp.sum(spread(terms, "dp", N_DP), axis=0)
    terms = spread(terms, ("ctx", "tp"), TEAM).reshape(N_CTX, N_TP, terms.shape[0])
    by_half = terms.transpose(1, 0, 2)
    vector_grad = jnp.concatenate(
        [by_half[:, :, part * FEAT : (part + 1) * FEAT].reshape(1, D) for part in range(3)]
        + [by_half[:, :, QKV : QKV + HIDDEN].reshape(FF // D, D)]
        + [
            terms[:, :, QKV + HIDDEN + part * FEAT : QKV + HIDDEN + (part + 1) * FEAT].reshape(1, D)
            for part in (0, 0, 1, 2)
        ],
        axis=0,
    )

    new_qkv = adam_update(w_qkv, sum_qkv, mom1_qkv, mom2_qkv, 2.0 / math.sqrt(D))
    new_out = adam_update(w_out, sum_out, mom1_out, mom2_out, 16.0 / math.sqrt(D))
    new_fc1 = adam_update(w_fc1, sum_fc1, mom1_fc1, mom2_fc1, 2.0 / math.sqrt(D))
    new_fc2 = adam_update(w_fc2, sum_fc2, mom1_fc2, mom2_fc2, 2.0 / math.sqrt(FF))
    new_vec = adam_update(vectors, vector_grad, mom1_vec, mom2_vec, 0.2)
    return (
        block_output,
        input_grad,
        new_qkv[0],
        new_out[0],
        new_fc1[0],
        new_fc2[0],
        new_vec[0],
        new_qkv[1],
        new_out[1],
        new_fc1[1],
        new_fc2[1],
        new_vec[1],
        new_qkv[2],
        new_out[2],
        new_fc1[2],
        new_fc2[2],
        new_vec[2],
    )


def solution(mesh):
    in_specs = (
        P(("dp", "ctx"), None),
        P(("dp", "ctx"), None),
        P("dp", "ctx"),
        P("dp", None),
        P(("dp", "ctx"), None, "tp"),
        P("tp", ("dp", "ctx"), None),
        P(("dp", "ctx"), "tp"),
        P("tp", ("dp", "ctx"), None),
        P(),
        P(("dp", "ctx"), None, "tp"),
        P("tp", ("dp", "ctx"), None),
        P(("dp", "ctx"), "tp"),
        P("tp", ("dp", "ctx"), None),
        P(),
        P(("dp", "ctx"), None, "tp"),
        P("tp", ("dp", "ctx"), None),
        P(("dp", "ctx"), "tp"),
        P("tp", ("dp", "ctx"), None),
        P(),
    )
    out_specs = (
        P(("dp", "ctx"), None),
        P(("dp", "ctx"), None),
        P(("dp", "ctx"), None, "tp"),
        P("tp", ("dp", "ctx"), None),
        P(("dp", "ctx"), "tp"),
        P("tp", ("dp", "ctx"), None),
        P(),
        P(("dp", "ctx"), None, "tp"),
        P("tp", ("dp", "ctx"), None),
        P(("dp", "ctx"), "tp"),
        P("tp", ("dp", "ctx"), None),
        P(),
        P(("dp", "ctx"), None, "tp"),
        P("tp", ("dp", "ctx"), None),
        P(("dp", "ctx"), "tp"),
        P("tp", ("dp", "ctx"), None),
        P(),
    )
    return jax.shard_map(shards, mesh=mesh, in_specs=in_specs, out_specs=out_specs, check_vma=False)
```

time: 5690 us -> 424 us (0.07)
  waiting for transfers between devices: 5410 us -> 162 us
  matrix products: 133 us -> 56 us
    all_gather x8 -> x2, waiting for transfers between devices: 2640 us -> 16.5 us  [the longest x1 16.5 us: shards(): w_in = lax.all_gather(columns, 'dp', axis=0, tiled=True)]
    reduce_scatter x4 -> x2, waiting for transfers between devices: 2360 us -> 0.02 us  [the longest x1 0.02 us: shards(): grad_fc1 = lax.psum_scatter(grad_fc1, 'dp', scatter_dimension=0, tiled=True)]
    ppermute x15 -> x9, waiting for transfers between devices: 223 us -> 0.84 us  [the longest x7 0.83 us: swap(): return lax.ppermute(value, 'tp', [(0, 1), (1, 0)])]
    psum x2 -> x0, waiting for transfers between devices: 182 us -> none  [the longest x1 115 us: shards(): vector_grad = lax.psum(vector_term, ('dp', 'ctx', 'tp'))]
    all_to_all x0 -> x11, waiting for transfers between devices: none -> 145 us  [the longest x5 70.7 us: spread(): lax.all_to_all(jnp.broadcast_to(value[None], (count,) + value.shape), axi...]
    dot_general x60 -> x10, matrix products: 133 us -> 56 us  [dot(): lax.dot_general(left, right, (dims, ((), ())), preferred_element_type=F32)]
    all_to_all x0 -> x11, starting transfers between devices: none -> 57.7 us  [the longest x5 24.3 us: spread(): lax.all_to_all(jnp.broadcast_to(value[None], (count,) + value.shape), axi...]
  transfers between devices with their start and end apart: 29 -> 24, of which waited for: 29 -> 13; matrix products, arithmetic and copies ran while one was open for 3% -> 21% of each run, Pallas kernels for 0% -> 0%
where the time goes in v1:
time: 424 us; the launch traced here: 416 us
  waiting for transfers between devices  162 us (38%)
  starting transfers between devices  68.5 us (16%)
  matrix products  56 us (13%)
  other arithmetic  37.6 us (9%)
  blocking collectives  36.9 us (9%)
  local copies, waits for them, and re-layouts  27.8 us (7%)
  between operations  15.2 us (4%)
  Pallas kernels  11.8 us (3%)
    all_to_all x5, waiting for transfers between devices, spread(): lax.all_to_all(jnp.broadcast_to(value[None], (count,) + value.shape), axi...  70.7 us
    dot_general x10, matrix products, dot(): lax.dot_general(left, right, (dims, ((), ())), preferred_element_type=F32)  56 us
    all_to_all x2, waiting for transfers between devices, to_owner(): lax.all_to_all(mine, 'ctx', 0, 0, tiled=True).astype(F32)  40 us
    all_to_all x1, blocking collectives, shards(): lax.all_to_all(columns.transpose(1, 0, 2), 'ctx', 0, 0, tiled=True)  36.9 us
    all_to_all x5, starting transfers between devices, spread(): lax.all_to_all(jnp.broadcast_to(value[None], (count,) + value.shape), axi...  24.3 us
    all_to_all x2, waiting for transfers between devices, summed(): pieces = lax.all_to_all(pieces, 'dp', 0, 0, tiled=True)  18.8 us
    all_gather x1, waiting for transfers between devices, shards(): w_in = lax.all_gather(columns, 'dp', axis=0, tiled=True)  16.5 us
    all_to_all x1, waiting for transfers between devices, shards(): lax.all_to_all(back_columns, 'ctx', 0, 0, tiled=True).astype(F32)  13.9 us
  transfers between devices with their start and end apart: 24, of which 13 were waited for; matrix products, arithmetic and copies ran while one was open for 21% of the time, Pallas kernels for 0%

profile of v1, /device:TPU:1, one launch (start us, length us, event | category | flops | bytes accessed | tf_op | source)
XLA Modules:
  0.0 416.0 jit_solution(12532160781137272843)
XLA Ops:
  11.3 36.9 %all_to_all.63 = bf16[8,32,896]{2,1,0:T(8,128)(2,1)} all-to-all(bf16[8,32,896]{2,1,0:T(8,128)(2,1)S(1)} %copy.107), channel_id=1, replica_groups=mesh['dp'=8,'ctx'=8,'tp'=2] {'ctx'}, dimensions={0} | all-to-all | bytes 917504 | tf_op jit(solution)/shard_map/all_to_all | solution.py:231
  49.8 4.5 %all-to-all-start.2 = ((bf16[8,64,2048]{2,1,0:T(8,128)(2,1)}), bf16[8,64,2048]{2,1,0:T(8,128)(2,1)}, u32[]{:S(2)}, u32[]{:S(2)}) async-start(bf16[8,64,2048]{2,1,0:T(8,128)(2,1)} %broadcast_in_dim.37), calls=%async_computation.2 | async-start | bytes 4194304 | tf_op jit(solution)/shard_map/all_to_all | solution.py:188
  55.5 30.0 %all-to-all-done.2 = bf16[8,64,2048]{2,1,0:T(8,128)(2,1)} async-done(((bf16[8,64,2048]{2,1,0:T(8,128)(2,1)}), bf16[8,64,2048]{2,1,0:T(8,128)(2,1)}, u32[]{:S(2)}, u32[]{:S(2)}) %all-to-all-start.2) | async-done | bytes 2097184 | tf_op jit(solution)/shard_map/all_to_all | solution.py:188
  87.2 4.8 %all-to-all-start = ((bf16[8,64,2048]{2,1,0:T(8,128)(2,1)}), bf16[8,64,2048]{2,1,0:T(8,128)(2,1)}, u32[]{:S(2)}, u32[]{:S(2)}) async-start(bf16[8,64,2048]{2,1,0:T(8,128)(2,1)} %broadcast_in_dim.36), calls=%async_computation | async-start | bytes 4194304 | tf_op jit(solution)/shard_map/all_to_all | solution.py:188
  94.8 26.0 %all-to-all-done = bf16[8,64,2048]{2,1,0:T(8,128)(2,1)} async-done(((bf16[8,64,2048]{2,1,0:T(8,128)(2,1)}), bf16[8,64,2048]{2,1,0:T(8,128)(2,1)}, u32[]{:S(2)}, u32[]{:S(2)}) %all-to-all-start) | async-done | bytes 2097184 | tf_op jit(solution)/shard_map/all_to_all | solution.py:188
  128.1 5.4 %all-to-all-done.3 = s32[8,1,64]{2,1,0:T(1,128)S(1)} async-done(((s32[8,1,64]{2,1,0:T(1,128)}), s32[8,1,64]{2,1,0:T(1,128)S(1)}, u32[]{:S(2)}, u32[]{:S(2)}) %all-to-all-start.3) | async-done | bytes 2080 | tf_op jit(solution)/shard_map/all_to_all | solution.py:188
  142.5 6.4 %fusion.8 = f32[1024,640]{1,0:T(8,128)S(1)} fusion(bf16[512,2048]{1,0:T(8,128)(2,1)S(1)} %bitcast.106, bf16[128,2048]{1,0:T(8,128)(2,1)S(1)} %bitcast.115, bf16[512,2048]{1,0:T(8,128)(2,1)} %collective-permute-done.1, bf16[512,2048]{1,0:T(8,128)(2,1)} %bitcast.6), kind=kOutput, calls=%fused_computation.37 | convolution fusion | flops 2697986048 | bytes 9437184 | tf_op jit(solution)/shard_map/dot_general | solution.py:63
  153.7 16.5 %all-gather.4.cloned.1.call-done = bf16[2048,896]{1,0:T(8,128)(2,1)} async-done(((bf16[256,896]{1,0:T(8,128)(2,1)}), bf16[2048,896]{1,0:T(8,128)(2,1)}) %all-gather.4.cloned.1.call-update) | async-done | bytes 3670032 | tf_op jit(solution)/shard_map/all_gather | solution.py:233
  170.1 7.2 %fusion = f32[1024,896]{0,1:T(8,128)S(1)} fusion(bf16[2048,896]{1,0:T(8,128)(2,1)} %all-gather.4.cloned.1.call-done, bf16[512,2048]{1,0:T(8,128)(2,1)} %collective-permute-done, bf16[512,2048]{1,0:T(8,128)(2,1)} %bitcast.2), kind=kOutput, calls=%fused_computation.24 | convolution fusion | flops 3766484992 | bytes 11534336 | tf_op jit(solution)/shard_map/dot_general | solution.py:63
  185.1 11.8 %shard_map.314 = (bf16[1024,128]{1,0:T(8,128)(2,1)S(1)}, bf16[1024,384]{1,0:T(8,128)(2,1)S(1)}, f32[8,384]{1,0:T(8,128)S(1)}) custom-call(f32[1024,384]{1,0:T(8,128)S(1)} %broadcast_add_fusion.pre_ref, bf16[1024,128]{1,0:T(8,128)(2,1)S(1)} %slice.196.dattn_ref, f32[1024,128]{1,0:T(8,128)S(1)} %get-tuple-element.69.cos_ref, ...), custom_call_target="tpu_custom_call" | custom-call | flops 1879048192 | bytes 8388608 | tf_op jit(solution)/shard_map/pallas_call | solution.py:158
  197.2 4.1 convert_reduce_fusion.4
  205.9 5.9 %convolution_convert_fusion = bf16[512,2048]{1,0:T(8,128)(2,1)} fusion(bf16[1024,512]{0,1:T(8,128)(2,1)S(1)} %get-tuple-element.45, bf16[512,2048]{1,0:T(8,128)(2,1)} %collective-permute-done.1, bf16[512,2048]{1,0:T(8,128)(2,1)} %bitcast.6), kind=kOutput, calls=%fused_computation.8 | convolution fusion | flops 2156920832 | bytes 7340032 | tf_op jit(solution)/shard_map/dot_general | solution.py:63
  211.8 3.8 convolution_convert_fusion.5
  219.1 6.5 %add_convert_fusion = bf16[512,2048]{1,0:T(8,128)(2,1)} fusion(bf16[512,2048]{1,0:T(8,128)(2,1)} %collective-permute-done.6, bf16[2048,896]{1,0:T(8,128)(2,1)} %all-gather.4.cloned.1.call-done, bf16[1024,384]{0,1:T(8,128)(2,1)S(1)} %copy.113, bf16[1024,512]{0,1:T(8,128)(2,1)S(1)} %get-tuple-element.32), kind=kOutput, calls=%fused_computation.5 | convolution fusion | flops 1884028928 | bytes 9699328 | tf_op jit(solution)/shard_map/dot_general | solution.py:63
  225.5 7.1 %all-to-all-done.8 = bf16[8,16,2048]{2,1,0:T(8,128)(2,1)S(1)} async-done(((bf16[8,16,2048]{2,1,0:T(8,128)(2,1)}), bf16[8,16,2048]{2,1,0:T(8,128)(2,1)S(1)}, u32[]{:S(2)}, u32[]{:S(2)}) %all-to-all-start.8) | async-done | bytes 524320 | tf_op jit(solution)/shard_map/all_to_all | solution.py:298
  233.4 6.0 %all-to-all-start.5 = ((bf16[8,64,2048]{2,1,0:T(8,128)(2,1)}), bf16[8,64,2048]{2,1,0:T(8,128)(2,1)S(1)}, u32[]{:S(2)}, u32[]{:S(2)}) async-start(bf16[8,64,2048]{2,1,0:T(8,128)(2,1)} %bitcast.110), calls=%async_computation.5 | async-start | bytes 4194304 | tf_op jit(solution)/shard_map/all_to_all | solution.py:326
  239.5 5.0 %convolution_convert_fusion.3 = bf16[512,2048]{1,0:T(8,128)(2,1)} fusion(bf16[512,2048]{1,0:T(8,128)(2,1)} %bitcast.107, bf16[128,2048]{1,0:T(8,128)(2,1)} %bitcast.116, bf16[1024,512]{0,1:T(8,128)(2,1)} %copy-done.16, bf16[1024,128]{0,1:T(8,128)(2,1)S(1)} %copy.111), kind=kOutput, calls=%fused_computation.11 | convolution fusion | flops 1349779456 | bytes 6029312 | tf_op jit(solution)/shard_map/dot_general | solution.py:63
  245.7 5.8 %convolution_convert_fusion.4 = bf16[2048,384]{1,0:T(8,128)(2,1)} fusion(bf16[1024,384]{1,0:T(8,128)(2,1)S(1)} %get-tuple-element.21, bf16[512,2048]{1,0:T(8,128)(2,1)} %collective-permute-done, bf16[512,2048]{1,0:T(8,128)(2,1)} %bitcast.2), kind=kOutput, calls=%fused_computation.12 | convolution fusion | flops 1619787776 | bytes 6553600 | tf_op jit(solution)/shard_map/dot_general | solution.py:63
  251.5 19.3 %all-to-all-done.5 = bf16[8,64,2048]{2,1,0:T(8,128)(2,1)S(1)} async-done(((bf16[8,64,2048]{2,1,0:T(8,128)(2,1)}), bf16[8,64,2048]{2,1,0:T(8,128)(2,1)S(1)}, u32[]{:S(2)}, u32[]{:S(2)}) %all-to-all-start.5) | async-done | bytes 2097184 | tf_op jit(solution)/shard_map/all_to_all | solution.py:326
  270.8 4.3 %all-to-all-start.6 = ((bf16[8,256,384]{2,1,0:T(8,128)(2,1)}), bf16[8,256,384]{2,1,0:T(8,128)(2,1)}, u32[]{:S(2)}, u32[]{:S(2)}) async-start(bf16[8,256,384]{2,1,0:T(8,128)(2,1)} %bitcast.112), calls=%async_computation.6 | async-start | bytes 3145728 | tf_op jit(solution)/shard_map/all_to_all | solution.py:298
  275.4 6.0 %convolution_convert_fusion.1 = bf16[2048,512]{1,0:T(8,128)(2,1)} fusion(bf16[1024,512]{0,1:T(8,128)(2,1)S(1)} %copy-done.18, bf16[512,2048]{1,0:T(8,128)(2,1)} %collective-permute-done, bf16[512,2048]{1,0:T(8,128)(2,1)} %bitcast.2), kind=kOutput, calls=%fused_computation.9 | convolution fusion | flops 2156920832 | bytes 7340032 | tf_op jit(solution)/shard_map/dot_general | solution.py:63
  284.0 11.7 %all-to-all-done.6 = bf16[8,256,384]{2,1,0:T(8,128)(2,1)} async-done(((bf16[8,256,384]{2,1,0:T(8,128)(2,1)}), bf16[8,256,384]{2,1,0:T(8,128)(2,1)}, u32[]{:S(2)}, u32[]{:S(2)}) %all-to-all-start.6) | async-done | bytes 1572896 | tf_op jit(solution)/shard_map/all_to_all | solution.py:298
  295.7 7.6 %all-to-all-start.9 = ((f32[16,2,128]{2,1,0:T(2,128)}), f32[16,2,128]{2,1,0:T(2,128)S(1)}, u32[]{:S(2)}, u32[]{:S(2)}) async-start(f32[16,2,128]{2,1,0:T(2,128)} %maximum_bitcast_fusion.1), calls=%async_computation.11 | async-start | bytes 32768 | tf_op jit(solution)/shard_map/all_to_all | solution.py:350
  303.3 5.8 %add_convert_fusion.1 = bf16[512,2048]{1,0:T(8,128)(2,1)} fusion(bf16[512,2048]{1,0:T(8,128)(2,1)} %collective-permute-done.4, bf16[512,2048]{1,0:T(8,128)(2,1)} %bitcast.108, bf16[128,2048]{1,0:T(8,128)(2,1)} %bitcast.117, bf16[1024,128]{0,1:T(8,128)(2,1)S(1)} %copy.111, bf16[1024,512]{0,1:T(8,128)(2,1)} %copy-done.16), kind=kOutput, calls=%fused_computation.7 | convolution fusion | flops 1351876608 | bytes 8126464 | tf_op jit(solution)/shard_map/dot_general | solution.py:63
  311.2 5.1 %all-to-all-start.4 = ((bf16[8,64,2048]{2,1,0:T(8,128)(2,1)}), bf16[8,64,2048]{2,1,0:T(8,128)(2,1)S(1)}, u32[]{:S(2)}, u32[]{:S(2)}) async-start(bf16[8,64,2048]{2,1,0:T(8,128)(2,1)} %bitcast.109), calls=%async_computation.4 | async-start | bytes 4194304 | tf_op jit(solution)/shard_map/all_to_all | solution.py:326
  326.6 20.6 %all-to-all-done.4 = bf16[8,64,2048]{2,1,0:T(8,128)(2,1)S(1)} async-done(((bf16[8,64,2048]{2,1,0:T(8,128)(2,1)}), bf16[8,64,2048]{2,1,0:T(8,128)(2,1)S(1)}, u32[]{:S(2)}, u32[]{:S(2)}) %all-to-all-start.4) | async-done | bytes 2097184 | tf_op jit(solution)/shard_map/all_to_all | solution.py:326
  347.8 4.7 %all-to-all-start.10 = ((f32[8,1,1280]{2,1,0:T(1,128)}), f32[8,1,1280]{2,1,0:T(1,128)}, u32[]{:S(2)}, u32[]{:S(2)}) async-start(f32[8,1,1280]{2,1,0:T(1,128)} %broadcast_in_dim.45), calls=%async_computation.12 | async-start | bytes 81920 | tf_op jit(solution)/shard_map/all_to_all | solution.py:188
  353.7 4.1 all-to-all-done.10
  359.2 7.0 %all-to-all-start.11 = ((f32[16,1,1280]{2,1,0:T(1,128)}), f32[16,1,1280]{2,1,0:T(1,128)S(1)}, u32[]{:S(2)}, u32[]{:S(2)}) async-start(f32[16,1,1280]{2,1,0:T(1,128)} %broadcast_in_dim.46), calls=%async_computation.13 | async-start | bytes 163840 | tf_op jit(solution)/shard_map/all_to_all | solution.py:188
  368.4 5.2 %all-to-all-done.11 = f32[16,1,1280]{2,1,0:T(1,128)S(1)} async-done(((f32[16,1,1280]{2,1,0:T(1,128)}), f32[16,1,1280]{2,1,0:T(1,128)S(1)}, u32[]{:S(2)}, u32[]{:S(2)}) %all-to-all-start.11) | async-done | bytes 81952 | tf_op jit(solution)/shard_map/all_to_all | solution.py:188
  378.4 7.0 %all-to-all-start.7 = ((bf16[8,32,896]{2,1,0:T(8,128)(2,1)}), bf16[8,32,896]{2,1,0:T(8,128)(2,1)S(1)}, u32[]{:S(2)}, u32[]{:S(2)}) async-start(bf16[8,32,896]{2,1,0:T(8,128)(2,1)} %bitcast.25), calls=%async_computation.8 | async-start | bytes 917504 | tf_op jit(solution)/shard_map/all_to_all | solution.py:308
  390.2 13.9 %all-to-all-done.7 = bf16[8,32,896]{2,1,0:T(8,128)(2,1)S(1)} async-done(((bf16[8,32,896]{2,1,0:T(8,128)(2,1)}), bf16[8,32,896]{2,1,0:T(8,128)(2,1)S(1)}, u32[]{:S(2)}, u32[]{:S(2)}) %all-to-all-start.7) | async-done | bytes 458784 | tf_op jit(solution)/shard_map/all_to_all | solution.py:308
  (225 shorter events, 85.1 us)
Async XLA Ops:
  7.2 116.0 %copy-start = (s32[1,128]{1,0:T(1,128)S(1)}, s32[1,128]{1,0:T(1,128)}, u32[]{:S(2)}) copy-start(s32[1,128]{1,0:T(1,128)} %param.21) | copy-start | bytes 1540
  7.2 132.0 %all-gather.6.cloned.1.call-start = ((), (), s32[]{:S(2)}) async-start(), calls=%async_computation.17 | async-start | bytes 2949120 | tf_op jit(solution)/shard_map/all_gather | solution.py:235
  9.4 0.7 collective-permute-start.2
  10.8 159.3 %all-gather.4.cloned.1.call-start = ((), (), s32[]{:S(2)}) async-start(), calls=%async_computation.14 | async-start | bytes 4128768 | tf_op jit(solution)/shard_map/all_gather | solution.py:233
  11.0 37.2 %copy-start.19 = (bf16[128,2048]{1,0:T(8,128)(2,1)S(1)}, bf16[128,2048]{1,0:T(8,128)(2,1)}, u32[]{:S(2)}) copy-start(bf16[128,2048]{1,0:T(8,128)(2,1)} %param.20) | copy-start | bytes 1572868
  49.8 35.8 %all-to-all-start.2 = ((bf16[8,64,2048]{2,1,0:T(8,128)(2,1)}), bf16[8,64,2048]{2,1,0:T(8,128)(2,1)}, u32[]{:S(2)}, u32[]{:S(2)}) async-start(bf16[8,64,2048]{2,1,0:T(8,128)(2,1)} %broadcast_in_dim.37), calls=%async_computation.2 | async-start | bytes 4194304 | tf_op jit(solution)/shard_map/all_to_all | solution.py:188
  54.4 32.7 %copy-start.37 = (f32[64]{0:T(128)}, f32[64]{0:T(128)S(1)}, u32[]{:S(2)}) copy-start(f32[64]{0:T(128)S(1)} %broadcast_multiply_fusion.2) | copy-start | bytes 772
  54.7 32.5 %copy-start.39 = (f32[64]{0:T(128)}, f32[64]{0:T(128)S(1)}, u32[]{:S(2)}) copy-start(f32[64]{0:T(128)S(1)} %add_rsqrt_fusion) | copy-start | bytes 772
  87.2 40.1 %copy-start.43 = (s32[1,4]{1,0:T(1,128)S(1)}, s32[1,4]{1,0:T(1,128)}, u32[]{:S(2)}) copy-start(s32[1,4]{1,0:T(1,128)} %param.22) | copy-start | bytes 52
  87.2 33.6 %all-to-all-start = ((bf16[8,64,2048]{2,1,0:T(8,128)(2,1)}), bf16[8,64,2048]{2,1,0:T(8,128)(2,1)}, u32[]{:S(2)}, u32[]{:S(2)}) async-start(bf16[8,64,2048]{2,1,0:T(8,128)(2,1)} %broadcast_in_dim.36), calls=%async_computation | async-start | bytes 4194304 | tf_op jit(solution)/shard_map/all_to_all | solution.py:188
  92.0 50.5 %collective-permute-start.1 = (bf16[512,2048]{1,0:T(8,128)(2,1)}, bf16[512,2048]{1,0:T(8,128)(2,1)}, u32[]{:S(2)}, u32[]{:S(2)}) collective-permute-start(bf16[512,2048]{1,0:T(8,128)(2,1)} %bitcast.6), channel_id=1, source_target_pairs={{0,1},{1,0},{2,3},{3,2},{4,5},{5,4},{6,7},{7,6},{8,9},{9,8},{10,11... | collective-permute-start | bytes 6291464 | tf_op jit(solution)/shard_map/ppermute | solution.py:184
  120.8 32.9 %collective-permute-start = (bf16[512,2048]{1,0:T(8,128)(2,1)}, bf16[512,2048]{1,0:T(8,128)(2,1)}, u32[]{:S(2)}, u32[]{:S(2)}) collective-permute-start(bf16[512,2048]{1,0:T(8,128)(2,1)} %bitcast.2), channel_id=1, source_target_pairs={{0,1},{1,0},{2,3},{3,2},{4,5},{5,4},{6,7},{7,6},{8,9},{9,8},{10,11... | collective-permute-start | bytes 6291464 | tf_op jit(solution)/shard_map/ppermute | solution.py:184
  123.8 9.7 %all-to-all-start.3 = ((s32[8,1,64]{2,1,0:T(1,128)}), s32[8,1,64]{2,1,0:T(1,128)S(1)}, u32[]{:S(2)}, u32[]{:S(2)}) async-start(s32[8,1,64]{2,1,0:T(1,128)} %broadcast_in_dim.38), calls=%async_computation.3 | async-start | bytes 8192 | tf_op jit(solution)/shard_map/all_to_all | solution.py:188
  127.2 247.8 %reduce-scatter.5.cloned.1.call-start = ((), (), s32[]{:S(2)}) async-start(), calls=%async_computation.16 | async-start | bytes 2359296 | tf_op jit(solution)/shard_map/reduce_scatter | solution.py:292
  134.8 2.0 collective-permute-start.3
  205.0 14.1 %collective-permute-start.6 = (bf16[512,2048]{1,0:T(8,128)(2,1)}, bf16[512,2048]{1,0:T(8,128)(2,1)}, u32[]{:S(2)}, u32[]{:S(2)}) collective-permute-start(bf16[512,2048]{1,0:T(8,128)(2,1)} %convolution_convert_fusion.2), channel_id=1, source_target_pairs={{0,1},{1,0},{2,3},{3,2},{4,5},{5,4},{6,7},{7,6},{8,9},{9,8},{10,11... | collective-permute-start | bytes 6291464 | tf_op jit(solution)/shard_map/ppermute | solution.py:184
  215.5 17.0 %all-to-all-start.8 = ((bf16[8,16,2048]{2,1,0:T(8,128)(2,1)}), bf16[8,16,2048]{2,1,0:T(8,128)(2,1)S(1)}, u32[]{:S(2)}, u32[]{:S(2)}) async-start(bf16[8,16,2048]{2,1,0:T(8,128)(2,1)} %bitcast.118), calls=%async_computation.9 | async-start | bytes 1048576 | tf_op jit(solution)/shard_map/all_to_all | solution.py:298
  233.4 37.5 %all-to-all-start.5 = ((bf16[8,64,2048]{2,1,0:T(8,128)(2,1)}), bf16[8,64,2048]{2,1,0:T(8,128)(2,1)S(1)}, u32[]{:S(2)}, u32[]{:S(2)}) async-start(bf16[8,64,2048]{2,1,0:T(8,128)(2,1)} %bitcast.110), calls=%async_computation.5 | async-start | bytes 4194304 | tf_op jit(solution)/shard_map/all_to_all | solution.py:326
  244.6 58.7 %collective-permute-start.4 = (bf16[512,2048]{1,0:T(8,128)(2,1)}, bf16[512,2048]{1,0:T(8,128)(2,1)}, u32[]{:S(2)}, u32[]{:S(2)}) collective-permute-start(bf16[512,2048]{1,0:T(8,128)(2,1)} %convolution_convert_fusion.3), channel_id=1, source_target_pairs={{0,1},{1,0},{2,3},{3,2},{4,5},{5,4},{6,7},{7,6},{8,9},{9,8},{10,11... | collective-permute-start | bytes 6291464 | tf_op jit(solution)/shard_map/ppermute | solution.py:184
  270.8 24.8 %all-to-all-start.6 = ((bf16[8,256,384]{2,1,0:T(8,128)(2,1)}), bf16[8,256,384]{2,1,0:T(8,128)(2,1)}, u32[]{:S(2)}, u32[]{:S(2)}) async-start(bf16[8,256,384]{2,1,0:T(8,128)(2,1)} %bitcast.112), calls=%async_computation.6 | async-start | bytes 3145728 | tf_op jit(solution)/shard_map/all_to_all | solution.py:298
  275.1 101.5 %reduce-scatter.3.cloned.1.call-start = ((), (), s32[]{:S(2)}) async-start(), calls=%async_computation.15 | async-start | bytes 2359296 | tf_op jit(solution)/shard_map/reduce_scatter | solution.py:290
  295.7 14.9 %all-to-all-start.9 = ((f32[16,2,128]{2,1,0:T(2,128)}), f32[16,2,128]{2,1,0:T(2,128)S(1)}, u32[]{:S(2)}, u32[]{:S(2)}) async-start(f32[16,2,128]{2,1,0:T(2,128)} %maximum_bitcast_fusion.1), calls=%async_computation.11 | async-start | bytes 32768 | tf_op jit(solution)/shard_map/all_to_all | solution.py:350
  311.2 36.0 %all-to-all-start.4 = ((bf16[8,64,2048]{2,1,0:T(8,128)(2,1)}), bf16[8,64,2048]{2,1,0:T(8,128)(2,1)S(1)}, u32[]{:S(2)}, u32[]{:S(2)}) async-start(bf16[8,64,2048]{2,1,0:T(8,128)(2,1)} %bitcast.109), calls=%async_computation.4 | async-start | bytes 4194304 | tf_op jit(solution)/shard_map/all_to_all | solution.py:326
  320.4 45.8 %copy-start.3 = (f32[64,2048]{1,0:T(8,128)S(1)}, f32[64,2048]{1,0:T(8,128)}, u32[]{:S(2)}) copy-start(f32[64,2048]{1,0:T(8,128)} %copy-done.2) | copy-start | bytes 1572868
  320.5 45.8 %copy-start.7 = (bf16[128,2048]{1,0:T(8,128)(2,1)S(1)}, bf16[128,2048]{1,0:T(8,128)(2,1)}, u32[]{:S(2)}) copy-start(bf16[128,2048]{1,0:T(8,128)(2,1)} %param.19) | copy-start | bytes 1572868
  326.6 39.7 %copy-start.41 = (f32[64]{0:T(128)S(1)}, f32[64]{0:T(128)}, u32[]{:S(2)}) copy-start(f32[64]{0:T(128)} %broadcast_multiply_fusion) | copy-start | bytes 772
  347.8 9.9 %all-to-all-start.10 = ((f32[8,1,1280]{2,1,0:T(1,128)}), f32[8,1,1280]{2,1,0:T(1,128)}, u32[]{:S(2)}, u32[]{:S(2)}) async-start(f32[8,1,1280]{2,1,0:T(1,128)} %broadcast_in_dim.45), calls=%async_computation.12 | async-start | bytes 81920 | tf_op jit(solution)/shard_map/all_to_all | solution.py:188
  359.2 14.4 %all-to-all-start.11 = ((f32[16,1,1280]{2,1,0:T(1,128)}), f32[16,1,1280]{2,1,0:T(1,128)S(1)}, u32[]{:S(2)}, u32[]{:S(2)}) async-start(f32[16,1,1280]{2,1,0:T(1,128)} %broadcast_in_dim.46), calls=%async_computation.13 | async-start | bytes 163840 | tf_op jit(solution)/shard_map/all_to_all | solution.py:188
  367.8 17.6 %collective-permute-start.5 = (bf16[64,2048]{1,0:T(8,128)(2,1)S(1)}, bf16[64,2048]{1,0:T(8,128)(2,1)S(1)}, u32[]{:S(2)}, u32[]{:S(2)}) collective-permute-start(bf16[64,2048]{1,0:T(8,128)(2,1)S(1)} %get-tuple-element.52), channel_id=1, source_target_pairs={{0,1},{1,0},{2,3},{3,2},{4,5},{5,4},{6,7},{7,6},{8,9},{9,8},{10,11... | collective-permute-start | bytes 786440 | tf_op jit(solution)/shard_map/ppermute | solution.py:184
  368.0 18.3 %collective-permute-start.7 = (f32[64,2048]{1,0:T(8,128)S(1)}, f32[64,2048]{1,0:T(8,128)S(1)}, u32[]{:S(2)}, u32[]{:S(2)}) collective-permute-start(f32[64,2048]{1,0:T(8,128)S(1)} %get-tuple-element.51), channel_id=1, source_target_pairs={{0,1},{1,0},{2,3},{3,2},{4,5},{5,4},{6,7},{7,6},{8,9},{9,8},{10,11... | collective-permute-start | bytes 1572872 | tf_op jit(solution)/shard_map/ppermute | solution.py:184
  375.9 11.5 %collective-permute-start.8 = (bf16[80,2048]{1,0:T(8,128)(2,1)S(1)}, bf16[80,2048]{1,0:T(8,128)(2,1)S(1)}, u32[]{:S(2)}, u32[]{:S(2)}) collective-permute-start(bf16[80,2048]{1,0:T(8,128)(2,1)S(1)} %pad_maximum_fusion.19), channel_id=1, source_target_pairs={{0,0},{2,16},{4,32},{6,48},{8,64},{10,80},{12,96},{14,112},{16,2},... | collective-permute-start | bytes 983048 | tf_op jit(solution)/shard_map/ppermute | solution.py:195
  378.4 25.7 %all-to-all-start.7 = ((bf16[8,32,896]{2,1,0:T(8,128)(2,1)}), bf16[8,32,896]{2,1,0:T(8,128)(2,1)S(1)}, u32[]{:S(2)}, u32[]{:S(2)}) async-start(bf16[8,32,896]{2,1,0:T(8,128)(2,1)} %bitcast.25), calls=%async_computation.8 | async-start | bytes 917504 | tf_op jit(solution)/shard_map/all_to_all | solution.py:308
  (36 other events, 218.3 us)
Sparse Core Ops, SparseCore 0:
  10.9 95.8 all-gather.5
  108.5 61.5 all-gather.3
  211.9 60.9 reduce-scatter.4
  281.6 50.4 reduce-scatter.2

commit v2 on v1

--- a/solution.py
+++ b/solution.py
@@ -184,15 +184,76 @@
     return lax.ppermute(value, "tp", [(0, 1), (1, 0)])
 
 
+PLACED = (0, 1, 3, 2, 4, 5, 7, 6)
+FLIPS = (4, 3, 1)
+
+
+def place_bits():
+    rank = lax.axis_index("dp")
+    high = (rank // 2) % 2
+    return (rank // 4, high, high ^ (rank % 2))
+
+
+def exchange(value, bit):
+    return lax.ppermute(value, "dp", [(d, d ^ FLIPS[bit]) for d in range(N_DP)])
+
+
+def gather_dp(values, order):
+    bits = place_bits()
+    values = [value[None, None, None] for value in values]
+    for bit in order:
+        first = bits[bit] == 0
+        grown = []
+        for value in values:
+            other = exchange(value, bit)
+            grown.append(
+                jnp.concatenate(
+                    [jnp.where(first, value, other), jnp.where(first, other, value)], axis=bit
+                )
+            )
+        values = grown
+    return [value.reshape((N_DP,) + value.shape[3:]) for value in values]
+
+
+def scatter_dp(values, order):
+    bits = place_bits()
+    values = [value.reshape((2, 2, 2) + value.shape[1:]) for value in values]
+    for bit in reversed(order):
+        rest = []
+        for value in values:
+            kept = lax.dynamic_slice_in_dim(value, bits[bit], 1, bit)
+            sent = lax.dynamic_slice_in_dim(value, 1 - bits[bit], 1, bit)
+            other = exchange(sent, bit)
+            rest.append((kept.astype(F32) + other.astype(F32)).astype(BF))
+        values = rest
+    return [value.reshape(value.shape[3:]) for value in values]
+
+
+def placed(value, axis):
+    shape = value.shape
+    blocks = value.reshape(shape[:axis] + (N_DP, shape[axis] // N_DP) + shape[axis + 1 :])
+    blocks = [lax.slice_in_dim(blocks, d, d + 1, axis=axis) for d in PLACED]
+    return jnp.concatenate(blocks, axis=axis).reshape(shape)
+
+
+def rows_to_team(value):
+    pairs = [
+        (d * N_CTX + c, PLACED[c] * N_CTX + d) for d in range(N_DP) for c in range(N_CTX)
+    ]
+    return lax.ppermute(value, ("dp", "ctx"), pairs)
+
+
+def rows_to_owner(value):
+    pairs = [
+        (PLACED[c] * N_CTX + d, d * N_CTX + c) for d in range(N_DP) for c in range(N_CTX)
+    ]
+    return lax.ppermute(value, ("dp", "ctx"), pairs)
+
+
 def spread(value, axis, count):
     return lax.all_to_all(
         jnp.broadcast_to(value[None], (count,) + value.shape), axis, 0, 0, tiled=True
     )
-
-
-def transposed(value):
-    pairs = [(a * N_CTX + b, b * N_CTX + a) for a in range(N_DP) for b in range(N_CTX)]
-    return lax.ppermute(value, ("dp", "ctx"), pairs)
 
 
 def shards(
@@ -218,10 +279,9 @@
 ):
     ctx_rank = lax.axis_index("ctx")
     tp_rank = lax.axis_index("tp")
-    team_rank = ctx_rank * N_TP + tp_rank
+    team_rank = tp_rank * N_CTX + ctx_rank
     own_d = D // (N_DP * N_CTX)
-    out_rows = w_out.shape[1]
-    fc2_rows = w_fc2.shape[1]
+    half_rows = N_CTX * HALF_ROWS
 
     columns = jnp.concatenate(
         [w_qkv[:, part].reshape(own_d, N_CTX, FEAT) for part in range(3)]
@@ -230,35 +290,44 @@
     ).astype(BF)
     columns = lax.all_to_all(columns.transpose(1, 0, 2), "ctx", 0, 0, tiled=True)
     columns = columns.reshape(N_CTX * own_d, QKV + HIDDEN)
-    w_in = lax.all_gather(columns, "dp", axis=0, tiled=True)
-    rows = transposed(jnp.concatenate([w_out[0], w_fc2[0]], axis=0).astype(BF))
-    rows = lax.all_gather(rows, "dp", axis=0, tiled=False)
-    w_back = jnp.concatenate(
-        [rows[:, :out_rows].reshape(FEAT, D), rows[:, out_rows:].reshape(HIDDEN, D)], axis=0
-    )
+    out_part = rows_to_team(w_out[0].astype(BF))
+    fc2_part = rows_to_team(w_fc2[0].astype(BF))
+    (mat_fc2,) = gather_dp([fc2_part], (2, 1, 0))
+    (mat_fc1,) = gather_dp([columns[:, QKV:]], (1, 0, 2))
+    mat_qkv, mat_out = gather_dp([columns[:, :QKV], out_part], (0, 2, 1))
+    mat_fc2 = mat_fc2.reshape(HIDDEN, D)
+    mat_out = mat_out.reshape(FEAT, D)
+    mat_fc1 = mat_fc1.reshape(D, HIDDEN)
+    mat_qkv = mat_qkv.reshape(D, QKV)
 
     def half(value, axis=0):
         return lax.dynamic_slice_in_dim(value, tp_rank * HALF_ROWS, HALF_ROWS, axis)
 
-    x_own = half(block_input).astype(F32)
+    x_own = placed(half(block_input), 1)
     dy_own = half(out_cotangent)
     tok_own = half(token_order[0])
-    row_mean = jnp.mean(x_own, axis=-1, keepdims=True)
-    centered = x_own - row_mean
-    inv_std = lax.rsqrt(jnp.mean(centered * centered, axis=-1, keepdims=True) + NORM_EPS)
-    normal_x = centered * inv_std
-    norm_gain = vectors[9]
-    norm_shift = vectors[10]
-    normed_own = (normal_x * norm_gain + norm_shift).astype(BF)
+    tok_pair = jnp.stack([tok_own // 32, tok_own % 32], axis=1).astype(BF)
+    x_wide = jnp.concatenate([x_own, jnp.pad(tok_pair, ((0, 0), (0, 126)))], axis=1)
 
     def whole_group(value):
-        mine = spread(value, "ctx", N_CTX)
-        mine = mine.reshape((N_CTX * HALF_ROWS,) + value.shape[1:])
+        mine = spread(value, "ctx", N_CTX).reshape(half_rows, value.shape[1])
         return jnp.concatenate([mine, swap(mine)], axis=0)
 
-    normed = whole_group(normed_own)
-    tok = whole_group(tok_own)
+    x_wide = whole_group(x_wide)
     dy = whole_group(dy_own)
+    tok_pair = x_wide[:, D : D + 2].astype(jnp.int32)
+    tok = tok_pair[:, 0] * 32 + tok_pair[:, 1]
+
+    def normal(value):
+        value = value.astype(F32)
+        centered = value - jnp.mean(value, axis=-1, keepdims=True)
+        inv_std = lax.rsqrt(jnp.mean(centered * centered, axis=-1, keepdims=True) + NORM_EPS)
+        return (centered * inv_std, inv_std)
+
+    norm_gain = placed(vectors[9], 0)
+    norm_shift = placed(vectors[10], 0)
+    normal_x = normal(x_wide[:, :D])[0]
+    normed = (normal_x * norm_gain + norm_shift).astype(BF)
 
     ends = jnp.cumsum(seq_lengths[0])
     starts = ends - seq_lengths[0]
@@ -272,37 +341,28 @@
     cos_table = jnp.cos(rotation)
     sin_table = jnp.sin(rotation) * jnp.where(lane < ROT // 2, -1.0, 1.0)
 
-    bias_qkv = lax.dynamic_slice(vectors, (0, tp_rank * (D // N_TP) + ctx_rank * FEAT), (3, FEAT))
-    bias_fc1 = lax.dynamic_slice_in_dim(
-        vectors[3:7].reshape(FF), tp_rank * (FF // N_TP) + ctx_rank * HIDDEN, HIDDEN
-    )
-    pre = dot(normed, w_in, ((1,), (0,)))
-    back = dot(dy, w_back, ((1,), (1,)))
-    hidden = pre[:, QKV:] + bias_fc1
-    pre_qkv = pre[:, :QKV] + bias_qkv.reshape(QKV)
+    bias_qkv = lax.dynamic_slice(vectors, (0, team_rank * FEAT), (3, FEAT))
+    bias_fc1 = lax.dynamic_slice_in_dim(vectors[3:7].reshape(FF), team_rank * HIDDEN, HIDDEN)
+    dattn = dot(dy, mat_out, ((1,), (1,))).astype(BF)
+    pre_qkv = dot(normed, mat_qkv, ((1,), (0,))) + bias_qkv.reshape(QKV)
+    hidden = dot(normed, mat_fc1, ((1,), (0,))) + bias_fc1
     active, slope = gelu_and_slope(hidden)
     active = active.astype(BF)
-    dhid = (back[:, FEAT:] * slope).astype(BF)
-    dattn = back[:, :FEAT].astype(BF)
+    dhid = (dot(dy, mat_fc2, ((1,), (1,))) * slope).astype(BF)
+
+    grad_fc2 = dot(active, dy, ((0,), (0,))).astype(BF)
+    grad_fc1 = dot(normed, dhid, ((0,), (0,))).astype(BF)
+    (grad_fc2,) = scatter_dp([grad_fc2.reshape(N_DP, HIDDEN // N_DP, D)], (2, 1, 0))
+    (grad_fc1,) = scatter_dp([grad_fc1.reshape(N_DP, D // N_DP, HIDDEN)], (1, 0, 2))
     attended, dpre, dpre_sums = attention(pre_qkv, dattn, cos_table, sin_table, tok, first)
-
-    grad_fc1 = dot(normed, dhid, ((0,), (0,))).astype(BF)
-    grad_fc1 = lax.psum_scatter(grad_fc1, "dp", scatter_dimension=0, tiled=True)
-    grad_fc2 = dot(active, dy, ((0,), (0,))).astype(BF)
-    grad_fc2 = lax.psum_scatter(grad_fc2, "dp", scatter_dimension=0, tiled=True)
+    grad_qkv = dot(normed, dpre, ((0,), (0,))).astype(BF)
     grad_out = dot(attended, dy, ((0,), (0,))).astype(BF)
-    grad_qkv = dot(normed, dpre, ((0,), (0,))).astype(BF)
-
-    def summed(value):
-        pieces = value.reshape((N_DP, value.shape[0] // N_DP) + value.shape[1:])
-        pieces = lax.all_to_all(pieces, "dp", 0, 0, tiled=True)
-        return jnp.sum(pieces.astype(F32), axis=0)
-
-    grad_qkv = summed(grad_qkv).astype(BF)
-    grad_out = summed(grad_out).astype(BF)
-    back_rows = transposed(jnp.concatenate([grad_out, grad_fc2], axis=0)).astype(F32)
-    sum_out = back_rows[None, :out_rows]
-    sum_fc2 = back_rows[None, out_rows:]
+    grad_qkv, grad_out = scatter_dp(
+        [grad_qkv.reshape(N_DP, D // N_DP, QKV), grad_out.reshape(N_DP, FEAT // N_DP, D)],
+        (0, 2, 1),
+    )
+    sum_out = rows_to_owner(grad_out).astype(F32)[None]
+    sum_fc2 = rows_to_owner(grad_fc2).astype(F32)[None]
     back_columns = jnp.concatenate([grad_qkv, grad_fc1], axis=1)
     back_columns = back_columns.reshape(N_CTX, own_d, QKV + HIDDEN)
     back_columns = lax.all_to_all(back_columns, "ctx", 0, 0, tiled=True).astype(F32)
@@ -317,13 +377,9 @@
     )
     sum_fc1 = back_columns[:, :, QKV:].transpose(1, 0, 2).reshape(own_d, N_CTX * HIDDEN)
 
-    def to_owner(left, right, dims):
-        rows_half = N_CTX * HALF_ROWS
-        theirs = dot(left[rows_half:], right, dims).astype(BF)
-        mine = dot(left[:rows_half], right, dims)
-        mine = (mine + swap(theirs).astype(F32)).astype(BF)
-        mine = mine.reshape(N_CTX, HALF_ROWS, D)
-        return jnp.sum(lax.all_to_all(mine, "ctx", 0, 0, tiled=True).astype(F32), axis=0)
+    def own_half(value):
+        mine = value[:half_rows].astype(F32) + swap(value[half_rows:].astype(BF)).astype(F32)
+        return mine.astype(BF).reshape(N_CTX, HALF_ROWS, D)
 
     def both_halves(value):
         other = swap(value)
@@ -332,41 +388,47 @@
             [jnp.where(first_core, value, other), jnp.where(first_core, other, value)], axis=0
         )
 
-    branch = to_owner(jnp.concatenate([attended, active], axis=1), w_back, ((1,), (0,)))
-    block_output = both_halves((x_own + branch + vectors[7] + vectors[8]).astype(BF))
-    normed_grad = to_owner(jnp.concatenate([dpre, dhid], axis=1), w_in, ((1,), (1,)))
+    normed_part = dot(dpre, mat_qkv, ((1,), (1,))) + dot(dhid, mat_fc1, ((1,), (1,)))
+    branch = dot(attended, mat_out, ((1,), (0,))) + dot(active, mat_fc2, ((1,), (0,)))
+    merged = jnp.concatenate([own_half(normed_part), own_half(branch)], axis=1)
+    merged = lax.all_to_all(merged, "ctx", 0, 0, tiled=True).astype(F32)
+    merged = jnp.sum(merged, axis=0)
+    normed_grad = merged[:HALF_ROWS]
+    branch = merged[HALF_ROWS:]
+    block_output = half(block_input).astype(F32) + branch + vectors[7] + vectors[8]
+    block_output = both_halves(block_output.astype(BF))
+    own_normal, inv_std = normal(x_own)
     scaled_grad = normed_grad * norm_gain
-    input_grad = dy_own.astype(F32) + inv_std * (
+    input_grad = inv_std * (
         scaled_grad
         - jnp.mean(scaled_grad, axis=-1, keepdims=True)
-        - normal_x * jnp.mean(scaled_grad * normal_x, axis=-1, keepdims=True)
-    )
-    input_grad = both_halves(input_grad)
-
+        - own_normal * jnp.mean(scaled_grad * own_normal, axis=-1, keepdims=True)
+    )
+    input_grad = both_halves(dy_own.astype(F32) + placed(input_grad, 1))
+
+    norm_terms = jnp.stack(
+        [jnp.sum(normed_part * normal_x, axis=0), jnp.sum(normed_part, axis=0)]
+    )
     dy_sum = jnp.sum(dy.astype(F32), axis=0)
     dy_sum = lax.dynamic_slice_in_dim(dy_sum, team_rank * FEAT, FEAT)
-    norm_terms = jnp.stack([jnp.sum(normed_grad * normal_x, axis=0), jnp.sum(normed_grad, axis=0)])
-    norm_terms = norm_terms.reshape(2, TEAM, FEAT).transpose(1, 0, 2)
-    norm_terms = jnp.sum(lax.all_to_all(norm_terms, ("ctx", "tp"), 0, 0, tiled=True), axis=0)
     terms = jnp.concatenate(
-        [
-            dpre_sums[0],
-            jnp.sum(dhid.astype(F32), axis=0),
-            dy_sum,
-            norm_terms.reshape(2 * FEAT),
-        ]
-    )
-    terms = jnp.sum(spread(terms, "dp", N_DP), axis=0)
-    terms = spread(terms, ("ctx", "tp"), TEAM).reshape(N_CTX, N_TP, terms.shape[0])
-    by_half = terms.transpose(1, 0, 2)
+        [dpre_sums[0], dy_sum, jnp.sum(dhid.astype(F32), axis=0), norm_terms.reshape(2 * D)]
+    ).reshape(40, 128)
+    for bit in range(3):
+        terms = terms + exchange(terms, bit)
+    whole = jnp.zeros((4, D), F32)
+    whole = lax.dynamic_update_slice(whole, terms[:4].reshape(4, FEAT), (0, team_rank * FEAT))
+    hidden_sums = lax.dynamic_update_slice_in_dim(
+        jnp.zeros((FF,), F32), terms[4:8].reshape(HIDDEN), team_rank * HIDDEN, 0
+    )
+    whole = jnp.concatenate(
+        [whole, hidden_sums.reshape(FF // D, D), terms[8:].reshape(2, D)], axis=0
+    )
+    for flip in (1, 2, 6):
+        whole = whole + lax.ppermute(whole, "ctx", [(c, c ^ flip) for c in range(N_CTX)])
+    whole = whole + swap(whole)
     vector_grad = jnp.concatenate(
-        [by_half[:, :, part * FEAT : (part + 1) * FEAT].reshape(1, D) for part in range(3)]
-        + [by_half[:, :, QKV : QKV + HIDDEN].reshape(FF // D, D)]
-        + [
-            terms[:, :, QKV + HIDDEN + part * FEAT : QKV + HIDDEN + (part + 1) * FEAT].reshape(1, D)
-            for part in (0, 0, 1, 2)
-        ],
-        axis=0,
+        [whole[:3], whole[4:8], whole[3:4], whole[3:4], placed(whole[8:], 1)], axis=0
     )
 
     new_qkv = adam_update(w_qkv, sum_qkv, mom1_qkv, mom2_qkv, 2.0 / math.sqrt(D))

time: 424 us -> 445 us (1.050)
  starting transfers between devices: 68.5 us -> 120 us
  blocking collectives: 36.9 us -> 0 us
  other arithmetic: 37.6 us -> 61 us
  matrix products: 56 us -> 38.4 us
  waiting for transfers between devices: 162 us -> 179 us
  between operations: 15.2 us -> 2.65 us
    ppermute x2 -> x34, waiting for transfers between devices: 0.01 us -> 130 us  [the longest x27 126 us: exchange(): return lax.ppermute(value, 'dp', [(d, d ^ FLIPS[bit]) for d in range(N_DP)])]
    all_to_all x5 -> x2, waiting for transfers between devices: 70.7 us -> 3.38 us  [spread(): lax.all_to_all(jnp.broadcast_to(value[None], (count,) + value.shape), axi...]
    ppermute x2 -> x34, starting transfers between devices: 1.36 us -> 63 us  [the longest x27 55.4 us: exchange(): return lax.ppermute(value, 'dp', [(d, d ^ FLIPS[bit]) for d in range(N_DP)])]
    all_to_all x1 -> x0, blocking collectives: 36.9 us -> none  [shards(): lax.all_to_all(columns.transpose(1, 0, 2), 'ctx', 0, 0, tiled=True)]
    dot_general x10 -> x12, matrix products: 56 us -> 38.4 us  [dot(): lax.dot_general(left, right, (dims, ((), ())), preferred_element_type=F32)]
    all_gather x2 -> x0, waiting for transfers between devices: 16.5 us -> none  [the longest x1 16.5 us: shards(): w_in = lax.all_gather(columns, 'dp', axis=0, tiled=True)]
    all_to_all x5 -> x2, waiting for transfers between devices: 60.3 us -> 44.4 us  [the longest x1 44.4 us: shards(): merged = lax.all_to_all(merged, 'ctx', 0, 0, tiled=True).astype(F32)]
    convert_element_type x2 -> x15, other arithmetic: 0.23 us -> 15.8 us  [the longest x2 7.14 us: own_half(): return mine.astype(BF).reshape(N_CTX, HALF_ROWS, D)]
  transfers between devices with their start and end apart: 24 -> 46, of which waited for: 13 -> 20; matrix products, arithmetic and copies ran while one was open for 21% -> 24% of each run, Pallas kernels for 0% -> 3%
where the time goes in v2:
time: 445 us; the launch traced here: 438 us
  waiting for transfers between devices  179 us (40%)
  starting transfers between devices  120 us (27%)
  other arithmetic  61 us (14%)
  matrix products  38.4 us (9%)
  local copies, waits for them, and re-layouts  24.7 us (6%)
  Pallas kernels  11.8 us (3%)
    ppermute x27, waiting for transfers between devices, exchange(): return lax.ppermute(value, 'dp', [(d, d ^ FLIPS[bit]) for d in range(N_DP)])  126 us
    ppermute x27, starting transfers between devices, exchange(): return lax.ppermute(value, 'dp', [(d, d ^ FLIPS[bit]) for d in range(N_DP)])  55.4 us
    all_to_all x1, waiting for transfers between devices, shards(): merged = lax.all_to_all(merged, 'ctx', 0, 0, tiled=True).astype(F32)  44.4 us
    dot_general x12, matrix products, dot(): lax.dot_general(left, right, (dims, ((), ())), preferred_element_type=F32)  38.4 us
    ppermute x7, starting transfers between devices, swap(): return lax.ppermute(value, 'tp', [(0, 1), (1, 0)])  19.2 us
    all_to_all x2, starting transfers between devices, spread(): lax.all_to_all(jnp.broadcast_to(value[None], (count,) + value.shape), axi...  14 us
    all_to_all x1, starting transfers between devices, shards(): lax.all_to_all(columns.transpose(1, 0, 2), 'ctx', 0, 0, tiled=True)  12 us
    pallas_call x1, Pallas kernels, attention(): pl.pallas_call(attention_kernel, grid=(tokens // Q_BLOCK,), out_shape=(ja...  11.8 us
  transfers between devices with their start and end apart: 46, of which 20 were waited for; matrix products, arithmetic and copies ran while one was open for 24% of the time, Pallas kernels for 3%

profile of v2, /device:TPU:1, one launch (start us, length us, event | category | flops | bytes accessed | tf_op | source)
XLA Modules:
  0.0 438.1 jit_solution(16947468305195014295)
XLA Ops:
  5.5 12.0 %all-to-all-start.1 = ((bf16[8,32,896]{2,1,0:T(8,128)(2,1)}), bf16[8,32,896]{2,1,0:T(8,128)(2,1)S(1)}, u32[]{:S(2)}, u32[]{:S(2)}) async-start(bf16[8,32,896]{2,1,0:T(8,128)(2,1)} %copy.63), calls=%async_computation.1 | async-start | bytes 917504 | tf_op jit(solution)/shard_map/all_to_all | solution.py:291
  29.6 6.7 %all-to-all-start = ((bf16[8,64,2176]{2,1,0:T(8,128)(2,1)}), bf16[8,64,2176]{2,1,0:T(8,128)(2,1)S(1)}, u32[]{:S(2)}, u32[]{:S(2)}) async-start(bf16[8,64,2176]{2,1,0:T(8,128)(2,1)} %broadcast_in_dim.38), calls=%async_computation | async-start | bytes 4456448 | tf_op jit(solution)/shard_map/all_to_all | solution.py:254
  39.6 25.3 %collective-permute-done.1 = bf16[1,1,1,256,384]{4,3,2,1,0:T(8,128)(2,1)S(1)} collective-permute-done((bf16[1,1,1,256,384]{4,3,2,1,0:T(8,128)(2,1)S(1)}, bf16[1,1,1,256,384]{4,3,2,1,0:T(8,128)(2,1)S(1)}, u32[]{:S(2)}, u32[]{:S(2)}) %collective-permute-start.1) | collective-permute-done | bytes 196640 | tf_op jit(solution)/shard_map/ppermute | solution.py:198
  73.5 7.4 %all-to-all-start.2 = ((bf16[8,64,2048]{2,1,0:T(8,128)(2,1)}), bf16[8,64,2048]{2,1,0:T(8,128)(2,1)}, u32[]{:S(2)}, u32[]{:S(2)}) async-start(bf16[8,64,2048]{2,1,0:T(8,128)(2,1)} %broadcast_in_dim.40), calls=%async_computation.2 | async-start | bytes 4194304 | tf_op jit(solution)/shard_map/all_to_all | solution.py:254
  90.3 14.7 %collective-permute-done.3 = bf16[2,1,2,256,384]{4,3,2,1,0:T(8,128)(2,1)S(1)} collective-permute-done((bf16[2,1,2,256,384]{4,3,2,1,0:T(8,128)(2,1)S(1)}, bf16[2,1,2,256,384]{4,3,2,1,0:T(8,128)(2,1)S(1)}, u32[]{:S(2)}, u32[]{:S(2)}) %collective-permute-start.3) | collective-permute-done | bytes 786464 | tf_op jit(solution)/shard_map/ppermute | solution.py:198
  106.4 3.4 all-to-all-done.2
  123.7 5.6 %convolution_convert_fusion = bf16[512,2048]{1,0:T(8,128)(2,1)S(1)} fusion(f32[1024,512]{1,0:T(8,128)S(1)} %fusion.65, f32[512]{0:T(512)S(1)} %copy-done.64, bf16[512,2048]{1,0:T(8,128)(2,1)S(1)} %collective-permute-done.4, bf16[512,2048]{1,0:T(8,128)(2,1)} %bitcast.7), kind=kOutput, calls=%fused_computation.25 | convolution fusion | flops 2162163712 | bytes 8390656 | tf_op jit(solution)/shard_map/dot_general | solution.py:63
  139.8 15.7 %collective-permute-done.30 = bf16[1,2,2,64,2048]{4,3,2,1,0:T(8,128)(2,1)} collective-permute-done((bf16[1,2,2,64,2048]{4,3,2,1,0:T(8,128)(2,1)}, bf16[1,2,2,64,2048]{4,3,2,1,0:T(8,128)(2,1)}, u32[]{:S(2)}, u32[]{:S(2)}) %collective-permute-start.30) | collective-permute-done | bytes 1048608 | tf_op jit(solution)/shard_map/ppermute | solution.py:198
  157.5 3.8 collective-permute-start.31
  161.3 4.5 %convolution_add_fusion.2.pre_ref = f32[1024,384]{1,0:T(8,128)S(1)} fusion(bf16[1024,2048]{1,0:T(8,128)(2,1)} %copy-done.6, bf16[2048,384]{1,0:T(8,128)(2,1)S(1)} %bitcast.171, f32[384]{0:T(512)S(1)} %copy-done.66), kind=kOutput, calls=%fused_computation.39 | convolution fusion | flops 1611005952 | bytes 7341568 | tf_op jit(solution)/shard_map/dot_general | solution.py:63
  165.8 6.1 %collective-permute-done.31 = bf16[1,1,2,64,2048]{4,3,2,1,0:T(8,128)(2,1)S(1)} collective-permute-done((bf16[1,1,2,64,2048]{4,3,2,1,0:T(8,128)(2,1)S(1)}, bf16[1,1,2,64,2048]{4,3,2,1,0:T(8,128)(2,1)S(1)}, u32[]{:S(2)}, u32[]{:S(2)}) %collective-permute-start.31) | collective-permute-done | bytes 524320 | tf_op jit(solution)/shard_map/ppermute | solution.py:198
  174.2 11.8 %shard_map.314 = (bf16[1024,128]{1,0:T(8,128)(2,1)S(1)}, bf16[1024,384]{1,0:T(8,128)(2,1)S(1)}, f32[8,384]{1,0:T(8,128)S(1)}) custom-call(f32[1024,384]{1,0:T(8,128)S(1)} %convolution_add_fusion.2.pre_ref, bf16[1024,128]{1,0:T(8,128)(2,1)S(1)} %convolution_convert_fusion.4.dattn_ref, f32[1024,128]{1,0:T(8,128)S(1)} %get-tuple-element.122.cos_ref, ...), custom_call_target="tpu_custom_call" | custom-call | flops 1879048192 | bytes 8388608 | tf_op jit(solution)/shard_map/pallas_call | solution.py:158
  189.3 4.5 %collective-permute-start.26 = (bf16[2,1,2,16,2048]{4,3,2,1,0:T(8,128)(2,1)S(1)}, bf16[2,1,2,16,2048]{4,3,2,1,0:T(8,128)(2,1)S(1)}, u32[]{:S(2)}, u32[]{:S(2)}) collective-permute-start(bf16[2,1,2,16,2048]{4,3,2,1,0:T(8,128)(2,1)S(1)} %constant_dynamic-slice_fusion.5), channel_id=1, source_target_pairs={{0,48},{16,32},{32,16},{48,0},{64,112},{80,96},{96,80},{112,64},{1... | collective-permute-start | bytes 786440 | tf_op jit(solution)/shard_map/ppermute | solution.py:198
  198.4 10.7 %collective-permute-start.20 = (bf16[2,1,2,256,384]{4,3,2,1,0:T(8,128)(2,1)S(1)}, bf16[2,1,2,256,384]{4,3,2,1,0:T(8,128)(2,1)S(1)}, u32[]{:S(2)}, u32[]{:S(2)}) collective-permute-start(bf16[2,1,2,256,384]{4,3,2,1,0:T(8,128)(2,1)S(1)} %constant_dynamic-slice_fusion.11), channel_id=1, source_target_pairs={{0,48},{16,32},{32,16},{48,0},{64,112},{80,96},{96,80},{112,64},{1... | collective-permute-start | bytes 2359304 | tf_op jit(solution)/shard_map/ppermute | solution.py:198
  209.1 12.8 %collective-permute-start.10 = (bf16[1,1,1,64,2048]{4,3,2,1,0:T(8,128)(2,1)S(1)}, bf16[1,1,1,64,2048]{4,3,2,1,0:T(8,128)(2,1)S(1)}, u32[]{:S(2)}, u32[]{:S(2)}) collective-permute-start(bf16[1,1,1,64,2048]{4,3,2,1,0:T(8,128)(2,1)S(1)} %bitcast.214), channel_id=1, source_target_pairs={{0,16},{16,0},{32,48},{48,32},{64,80},{80,64},{96,112},{112,96},{1... | collective-permute-start | bytes 786440 | tf_op jit(solution)/shard_map/ppermute | solution.py:198
  222.1 5.4 %collective-permute-done.10 = bf16[1,1,1,64,2048]{4,3,2,1,0:T(8,128)(2,1)S(1)} collective-permute-done((bf16[1,1,1,64,2048]{4,3,2,1,0:T(8,128)(2,1)S(1)}, bf16[1,1,1,64,2048]{4,3,2,1,0:T(8,128)(2,1)S(1)}, u32[]{:S(2)}, u32[]{:S(2)}) %collective-permute-start.10) | collective-permute-done | bytes 262176 | tf_op jit(solution)/shard_map/ppermute | solution.py:198
  230.4 8.8 %collective-permute-done.11 = bf16[1,1,2,64,2048]{4,3,2,1,0:T(8,128)(2,1)S(1)} collective-permute-done((bf16[1,1,2,64,2048]{4,3,2,1,0:T(8,128)(2,1)S(1)}, bf16[1,1,2,64,2048]{4,3,2,1,0:T(8,128)(2,1)S(1)}, u32[]{:S(2)}, u32[]{:S(2)}) %collective-permute-start.11) | collective-permute-done | bytes 524320 | tf_op jit(solution)/shard_map/ppermute | solution.py:198
  239.4 9.2 %collective-permute-start.12 = (bf16[1,2,2,64,2048]{4,3,2,1,0:T(8,128)(2,1)S(1)}, bf16[1,2,2,64,2048]{4,3,2,1,0:T(8,128)(2,1)S(1)}, u32[]{:S(2)}, u32[]{:S(2)}) collective-permute-start(bf16[1,2,2,64,2048]{4,3,2,1,0:T(8,128)(2,1)S(1)} %pad_maximum_fusion.5), channel_id=1, source_target_pairs={{0,64},{16,80},{32,96},{48,112},{64,0},{80,16},{96,32},{112,48},{1... | collective-permute-start | bytes 3145736 | tf_op jit(solution)/shard_map/ppermute | solution.py:198
  252.2 6.3 %collective-permute-done.21 = bf16[2,1,1,256,384]{4,3,2,1,0:T(8,128)(2,1)S(1)} collective-permute-done((bf16[2,1,1,256,384]{4,3,2,1,0:T(8,128)(2,1)S(1)}, bf16[2,1,1,256,384]{4,3,2,1,0:T(8,128)(2,1)S(1)}, u32[]{:S(2)}, u32[]{:S(2)}) %collective-permute-start.21) | collective-permute-done | bytes 393248 | tf_op jit(solution)/shard_map/ppermute | solution.py:198
  259.7 13.9 %collective-permute-done.12 = bf16[1,2,2,64,2048]{4,3,2,1,0:T(8,128)(2,1)S(1)} collective-permute-done((bf16[1,2,2,64,2048]{4,3,2,1,0:T(8,128)(2,1)S(1)}, bf16[1,2,2,64,2048]{4,3,2,1,0:T(8,128)(2,1)S(1)}, u32[]{:S(2)}, u32[]{:S(2)}) %collective-permute-start.12) | collective-permute-done | bytes 1048608 | tf_op jit(solution)/shard_map/ppermute | solution.py:198
  276.0 5.0 %convert_reduce_fusion.3 = (f32[512]{0:T(512)S(1)}, bf16[1024,512]{1,0:T(8,128)(2,1)S(1)}) fusion(f32[1024,512]{1,0:T(8,128)S(1)} %copy-done.76, f32[512]{0:T(512)S(1)} %copy-done.65, bf16[512,2048]{1,0:T(8,128)(2,1)S(1)} %bitcast.191, bf16[512,2048]{1,0:T(8,128)(2,1)S(1)} %copy-done.16, bf16[512,2048]{1,0:T(8,128)(2,1)} %bitcast.7), kind=kOutput, calls=%fused_computation.31 | convolution fusion | flops 2166881792 | bytes 9441280 | tf_op jit(solution)/shard_map/dot_general | solution.py:63
  294.1 4.1 fusion.47
  301.6 4.0 collective-permute-start.17
  305.9 8.7 %collective-permute-done.36 = f32[40,128]{1,0:T(8,128)S(1)} collective-permute-done((f32[40,128]{1,0:T(8,128)S(1)}, f32[40,128]{1,0:T(8,128)S(1)}, u32[]{:S(2)}, u32[]{:S(2)}) %collective-permute-start.36) | collective-permute-done | bytes 20512 | tf_op jit(solution)/shard_map/ppermute | solution.py:198
  314.6 3.5 collective-permute-start.16
  319.5 13.6 %collective-permute-done.24 = bf16[1,2,1,256,512]{4,3,2,1,0:T(8,128)(2,1)} collective-permute-done((bf16[1,2,1,256,512]{4,3,2,1,0:T(8,128)(2,1)}, bf16[1,2,1,256,512]{4,3,2,1,0:T(8,128)(2,1)}, u32[]{:S(2)}, u32[]{:S(2)}) %collective-permute-start.24) | collective-permute-done | bytes 524320 | tf_op jit(solution)/shard_map/ppermute | solution.py:198
  347.1 5.4 %all-to-all-start.4 = ((bf16[8,32,896]{2,1,0:T(8,128)(2,1)}), bf16[8,32,896]{2,1,0:T(8,128)(2,1)S(1)}, u32[]{:S(2)}, u32[]{:S(2)}) async-start(bf16[8,32,896]{2,1,0:T(8,128)(2,1)} %pad_maximum_fusion.13), calls=%async_computation.4 | async-start | bytes 917504 | tf_op jit(solution)/shard_map/all_to_all | solution.py:368
  352.5 3.6 fusion.9
  356.1 3.6 fusion.10
  362.3 6.8 %all-to-all-start.3 = ((bf16[8,128,2048]{2,1,0:T(8,128)(2,1)}), bf16[8,128,2048]{2,1,0:T(8,128)(2,1)}, u32[]{:S(2)}, u32[]{:S(2)}) async-start(bf16[8,128,2048]{2,1,0:T(8,128)(2,1)} %pad_maximum_fusion.1), calls=%async_computation.3 | async-start | bytes 8388608 | tf_op jit(solution)/shard_map/all_to_all | solution.py:394
  370.2 3.7 collective-permute-start.40
  382.6 44.4 %all-to-all-done.3 = bf16[8,128,2048]{2,1,0:T(8,128)(2,1)} async-done(((bf16[8,128,2048]{2,1,0:T(8,128)(2,1)}), bf16[8,128,2048]{2,1,0:T(8,128)(2,1)}, u32[]{:S(2)}, u32[]{:S(2)}) %all-to-all-start.3) | async-done | bytes 4194336 | tf_op jit(solution)/shard_map/all_to_all | solution.py:394
  (399 shorter events, 140.6 us)
Async XLA Ops:
  1.6 20.6 %collective-permute-start.5 = (bf16[16,2048]{1,0:T(8,128)(2,1)S(1)}, bf16[16,2048]{1,0:T(8,128)(2,1)S(1)}, u32[]{:S(2)}, u32[]{:S(2)}) collective-permute-start(bf16[16,2048]{1,0:T(8,128)(2,1)S(1)} %convert_bitcast_fusion.1), channel_id=1, source_target_pairs={{0,0},{2,16},{4,48},{6,32},{8,64},{10,80},{12,112},{14,96},{16,2},... | collective-permute-start | bytes 196616 | tf_op jit(solution)/shard_map/ppermute | solution.py:243
  5.5 22.4 %all-to-all-start.1 = ((bf16[8,32,896]{2,1,0:T(8,128)(2,1)}), bf16[8,32,896]{2,1,0:T(8,128)(2,1)S(1)}, u32[]{:S(2)}, u32[]{:S(2)}) async-start(bf16[8,32,896]{2,1,0:T(8,128)(2,1)} %copy.63), calls=%async_computation.1 | async-start | bytes 917504 | tf_op jit(solution)/shard_map/all_to_all | solution.py:291
  29.6 41.4 %all-to-all-start = ((bf16[8,64,2176]{2,1,0:T(8,128)(2,1)}), bf16[8,64,2176]{2,1,0:T(8,128)(2,1)S(1)}, u32[]{:S(2)}, u32[]{:S(2)}) async-start(bf16[8,64,2176]{2,1,0:T(8,128)(2,1)} %broadcast_in_dim.38), calls=%async_computation | async-start | bytes 4456448 | tf_op jit(solution)/shard_map/all_to_all | solution.py:254
  38.3 26.6 %collective-permute-start.1 = (bf16[1,1,1,256,384]{4,3,2,1,0:T(8,128)(2,1)S(1)}, bf16[1,1,1,256,384]{4,3,2,1,0:T(8,128)(2,1)S(1)}, u32[]{:S(2)}, u32[]{:S(2)}) collective-permute-start(bf16[1,1,1,256,384]{4,3,2,1,0:T(8,128)(2,1)S(1)} %slice_bitcast_fusion.2), channel_id=1, source_target_pairs={{0,64},{16,80},{32,96},{48,112},{64,0},{80,16},{96,32},{112,48},{1... | collective-permute-start | bytes 589832 | tf_op jit(solution)/shard_map/ppermute | solution.py:198
  38.8 28.4 %collective-permute-start.13 = (bf16[1,1,1,256,512]{4,3,2,1,0:T(8,128)(2,1)S(1)}, bf16[1,1,1,256,512]{4,3,2,1,0:T(8,128)(2,1)S(1)}, u32[]{:S(2)}, u32[]{:S(2)}) collective-permute-start(bf16[1,1,1,256,512]{4,3,2,1,0:T(8,128)(2,1)S(1)} %slice_bitcast_fusion.1), channel_id=1, source_target_pairs={{0,48},{16,32},{32,16},{48,0},{64,112},{80,96},{96,80},{112,64},{1... | collective-permute-start | bytes 786440 | tf_op jit(solution)/shard_map/ppermute | solution.py:198
  65.8 17.4 %collective-permute-start.2 = (bf16[2,1,1,256,384]{4,3,2,1,0:T(8,128)(2,1)}, bf16[2,1,1,256,384]{4,3,2,1,0:T(8,128)(2,1)}, u32[]{:S(2)}, u32[]{:S(2)}) collective-permute-start(bf16[2,1,1,256,384]{4,3,2,1,0:T(8,128)(2,1)} %pad_maximum_fusion.14), channel_id=1, source_target_pairs={{0,16},{16,0},{32,48},{48,32},{64,80},{80,64},{96,112},{112,96},{1... | collective-permute-start | bytes 1179656 | tf_op jit(solution)/shard_map/ppermute | solution.py:198
  68.2 18.0 %collective-permute-start.14 = (bf16[1,2,1,256,512]{4,3,2,1,0:T(8,128)(2,1)}, bf16[1,2,1,256,512]{4,3,2,1,0:T(8,128)(2,1)}, u32[]{:S(2)}, u32[]{:S(2)}) collective-permute-start(bf16[1,2,1,256,512]{4,3,2,1,0:T(8,128)(2,1)} %pad_maximum_fusion.11), channel_id=1, source_target_pairs={{0,64},{16,80},{32,96},{48,112},{64,0},{80,16},{96,32},{112,48},{1... | collective-permute-start | bytes 1572872 | tf_op jit(solution)/shard_map/ppermute | solution.py:198
  69.9 18.5 %collective-permute-start.8 = (bf16[2,1,2,16,2048]{4,3,2,1,0:T(8,128)(2,1)}, bf16[2,1,2,16,2048]{4,3,2,1,0:T(8,128)(2,1)}, u32[]{:S(2)}, u32[]{:S(2)}) collective-permute-start(bf16[2,1,2,16,2048]{4,3,2,1,0:T(8,128)(2,1)} %pad_maximum_fusion.16), channel_id=1, source_target_pairs={{0,48},{16,32},{32,16},{48,0},{64,112},{80,96},{96,80},{112,64},{1... | collective-permute-start | bytes 786440 | tf_op jit(solution)/shard_map/ppermute | solution.py:198
  73.5 36.4 %all-to-all-start.2 = ((bf16[8,64,2048]{2,1,0:T(8,128)(2,1)}), bf16[8,64,2048]{2,1,0:T(8,128)(2,1)}, u32[]{:S(2)}, u32[]{:S(2)}) async-start(bf16[8,64,2048]{2,1,0:T(8,128)(2,1)} %broadcast_in_dim.40), calls=%async_computation.2 | async-start | bytes 4194304 | tf_op jit(solution)/shard_map/all_to_all | solution.py:254
  80.8 33.9 %collective-permute-start = (bf16[512,2176]{1,0:T(8,128)(2,1)S(1)}, bf16[512,2176]{1,0:T(8,128)(2,1)}, u32[]{:S(2)}, u32[]{:S(2)}) collective-permute-start(bf16[512,2176]{1,0:T(8,128)(2,1)S(1)} %bitcast.166), channel_id=1, source_target_pairs={{0,1},{1,0},{2,3},{3,2},{4,5},{5,4},{6,7},{7,6},{8,9},{9,8},{10,11... | collective-permute-start | bytes 6684680 | tf_op jit(solution)/shard_map/ppermute | solution.py:184
  84.4 20.5 %collective-permute-start.3 = (bf16[2,1,2,256,384]{4,3,2,1,0:T(8,128)(2,1)S(1)}, bf16[2,1,2,256,384]{4,3,2,1,0:T(8,128)(2,1)S(1)}, u32[]{:S(2)}, u32[]{:S(2)}) collective-permute-start(bf16[2,1,2,256,384]{4,3,2,1,0:T(8,128)(2,1)S(1)} %pad_maximum_fusion.8), channel_id=1, source_target_pairs={{0,48},{16,32},{32,16},{48,0},{64,112},{80,96},{96,80},{112,64},{1... | collective-permute-start | bytes 2359304 | tf_op jit(solution)/shard_map/ppermute | solution.py:198
  88.4 24.7 %collective-permute-start.15 = (bf16[2,2,1,256,512]{4,3,2,1,0:T(8,128)(2,1)}, bf16[2,2,1,256,512]{4,3,2,1,0:T(8,128)(2,1)}, u32[]{:S(2)}, u32[]{:S(2)}) collective-permute-start(bf16[2,2,1,256,512]{4,3,2,1,0:T(8,128)(2,1)} %pad_maximum_fusion.6), channel_id=1, source_target_pairs={{0,16},{16,0},{32,48},{48,32},{64,80},{80,64},{96,112},{112,96},{1... | collective-permute-start | bytes 3145736 | tf_op jit(solution)/shard_map/ppermute | solution.py:198
  109.8 13.8 %collective-permute-start.4 = (bf16[512,2048]{1,0:T(8,128)(2,1)}, bf16[512,2048]{1,0:T(8,128)(2,1)S(1)}, u32[]{:S(2)}, u32[]{:S(2)}) collective-permute-start(bf16[512,2048]{1,0:T(8,128)(2,1)} %bitcast.7), channel_id=1, source_target_pairs={{0,1},{1,0},{2,3},{3,2},{4,5},{5,4},{6,7},{7,6},{8,9},{9,8},{10,11... | collective-permute-start | bytes 6291464 | tf_op jit(solution)/shard_map/ppermute | solution.py:184
  131.7 23.8 %collective-permute-start.30 = (bf16[1,2,2,64,2048]{4,3,2,1,0:T(8,128)(2,1)}, bf16[1,2,2,64,2048]{4,3,2,1,0:T(8,128)(2,1)}, u32[]{:S(2)}, u32[]{:S(2)}) collective-permute-start(bf16[1,2,2,64,2048]{4,3,2,1,0:T(8,128)(2,1)} %constant_dynamic-slice_fusion.2), channel_id=1, source_target_pairs={{0,64},{16,80},{32,96},{48,112},{64,0},{80,16},{96,32},{112,48},{1... | collective-permute-start | bytes 3145736 | tf_op jit(solution)/shard_map/ppermute | solution.py:198
  157.5 14.5 %collective-permute-start.31 = (bf16[1,1,2,64,2048]{4,3,2,1,0:T(8,128)(2,1)S(1)}, bf16[1,1,2,64,2048]{4,3,2,1,0:T(8,128)(2,1)S(1)}, u32[]{:S(2)}, u32[]{:S(2)}) collective-permute-start(bf16[1,1,2,64,2048]{4,3,2,1,0:T(8,128)(2,1)S(1)} %constant_dynamic-slice_fusion.1), channel_id=1, source_target_pairs={{0,48},{16,32},{32,16},{48,0},{64,112},{80,96},{96,80},{112,64},{1... | collective-permute-start | bytes 1572872 | tf_op jit(solution)/shard_map/ppermute | solution.py:198
  172.1 13.8 %collective-permute-start.32 = (bf16[1,1,1,64,2048]{4,3,2,1,0:T(8,128)(2,1)S(1)}, bf16[1,1,1,64,2048]{4,3,2,1,0:T(8,128)(2,1)S(1)}, u32[]{:S(2)}, u32[]{:S(2)}) collective-permute-start(bf16[1,1,1,64,2048]{4,3,2,1,0:T(8,128)(2,1)S(1)} %constant_dynamic-slice_fusion), channel_id=1, source_target_pairs={{0,16},{16,0},{32,48},{48,32},{64,80},{80,64},{96,112},{112,96},{1... | collective-permute-start | bytes 786440 | tf_op jit(solution)/shard_map/ppermute | solution.py:198
  189.3 32.7 %collective-permute-start.26 = (bf16[2,1,2,16,2048]{4,3,2,1,0:T(8,128)(2,1)S(1)}, bf16[2,1,2,16,2048]{4,3,2,1,0:T(8,128)(2,1)S(1)}, u32[]{:S(2)}, u32[]{:S(2)}) collective-permute-start(bf16[2,1,2,16,2048]{4,3,2,1,0:T(8,128)(2,1)S(1)} %constant_dynamic-slice_fusion.5), channel_id=1, source_target_pairs={{0,48},{16,32},{32,16},{48,0},{64,112},{80,96},{96,80},{112,64},{1... | collective-permute-start | bytes 786440 | tf_op jit(solution)/shard_map/ppermute | solution.py:198
  195.2 13.9 %collective-permute-start.9 = (bf16[64,2048]{1,0:T(8,128)(2,1)S(1)}, bf16[64,2048]{1,0:T(8,128)(2,1)S(1)}, u32[]{:S(2)}, u32[]{:S(2)}) collective-permute-start(bf16[64,2048]{1,0:T(8,128)(2,1)S(1)} %get-tuple-element.71), channel_id=1, source_target_pairs={{0,0},{2,16},{4,48},{6,32},{8,64},{10,80},{12,112},{14,96},{16,2},... | collective-permute-start | bytes 786440 | tf_op jit(solution)/shard_map/ppermute | solution.py:243
  198.4 50.3 %collective-permute-start.20 = (bf16[2,1,2,256,384]{4,3,2,1,0:T(8,128)(2,1)S(1)}, bf16[2,1,2,256,384]{4,3,2,1,0:T(8,128)(2,1)S(1)}, u32[]{:S(2)}, u32[]{:S(2)}) collective-permute-start(bf16[2,1,2,256,384]{4,3,2,1,0:T(8,128)(2,1)S(1)} %constant_dynamic-slice_fusion.11), channel_id=1, source_target_pairs={{0,48},{16,32},{32,16},{48,0},{64,112},{80,96},{96,80},{112,64},{1... | collective-permute-start | bytes 2359304 | tf_op jit(solution)/shard_map/ppermute | solution.py:198
  209.1 18.4 %collective-permute-start.10 = (bf16[1,1,1,64,2048]{4,3,2,1,0:T(8,128)(2,1)S(1)}, bf16[1,1,1,64,2048]{4,3,2,1,0:T(8,128)(2,1)S(1)}, u32[]{:S(2)}, u32[]{:S(2)}) collective-permute-start(bf16[1,1,1,64,2048]{4,3,2,1,0:T(8,128)(2,1)S(1)} %bitcast.214), channel_id=1, source_target_pairs={{0,16},{16,0},{32,48},{48,32},{64,80},{80,64},{96,112},{112,96},{1... | collective-permute-start | bytes 786440 | tf_op jit(solution)/shard_map/ppermute | solution.py:198
  230.3 19.1 %collective-permute-start.28 = (bf16[1,1,1,16,2048]{4,3,2,1,0:T(8,128)(2,1)S(1)}, bf16[1,1,1,16,2048]{4,3,2,1,0:T(8,128)(2,1)S(1)}, u32[]{:S(2)}, u32[]{:S(2)}) collective-permute-start(bf16[1,1,1,16,2048]{4,3,2,1,0:T(8,128)(2,1)S(1)} %constant_dynamic-slice_fusion.3), channel_id=1, source_target_pairs={{0,64},{16,80},{32,96},{48,112},{64,0},{80,16},{96,32},{112,48},{1... | collective-permute-start | bytes 196616 | tf_op jit(solution)/shard_map/ppermute | solution.py:198
  239.4 34.1 %collective-permute-start.12 = (bf16[1,2,2,64,2048]{4,3,2,1,0:T(8,128)(2,1)S(1)}, bf16[1,2,2,64,2048]{4,3,2,1,0:T(8,128)(2,1)S(1)}, u32[]{:S(2)}, u32[]{:S(2)}) collective-permute-start(bf16[1,2,2,64,2048]{4,3,2,1,0:T(8,128)(2,1)S(1)} %pad_maximum_fusion.5), channel_id=1, source_target_pairs={{0,64},{16,80},{32,96},{48,112},{64,0},{80,16},{96,32},{112,48},{1... | collective-permute-start | bytes 3145736 | tf_op jit(solution)/shard_map/ppermute | solution.py:198
  250.1 123.8 %collective-permute-start.29 = (bf16[16,2048]{1,0:T(8,128)(2,1)}, bf16[16,2048]{1,0:T(8,128)(2,1)}, u32[]{:S(2)}, u32[]{:S(2)}) collective-permute-start(bf16[16,2048]{1,0:T(8,128)(2,1)} %fusion.33), channel_id=1, source_target_pairs={{0,0},{16,2},{48,4},{32,6},{64,8},{80,10},{112,12},{96,14},{2,16},... | collective-permute-start | bytes 196616 | tf_op jit(solution)/shard_map/ppermute | solution.py:250
  259.3 80.2 %collective-permute-start.22 = (bf16[1,1,1,256,384]{4,3,2,1,0:T(8,128)(2,1)}, bf16[1,1,1,256,384]{4,3,2,1,0:T(8,128)(2,1)}, u32[]{:S(2)}, u32[]{:S(2)}) collective-permute-start(bf16[1,1,1,256,384]{4,3,2,1,0:T(8,128)(2,1)} %constant_dynamic-slice_fusion.9), channel_id=1, source_target_pairs={{0,64},{16,80},{32,96},{48,112},{64,0},{80,16},{96,32},{112,48},{1... | collective-permute-start | bytes 589832 | tf_op jit(solution)/shard_map/ppermute | solution.py:198
  292.0 26.1 %collective-permute-start.23 = (bf16[2,2,1,256,512]{4,3,2,1,0:T(8,128)(2,1)S(1)}, bf16[2,2,1,256,512]{4,3,2,1,0:T(8,128)(2,1)S(1)}, u32[]{:S(2)}, u32[]{:S(2)}) collective-permute-start(bf16[2,2,1,256,512]{4,3,2,1,0:T(8,128)(2,1)S(1)} %constant_dynamic-slice_fusion.8), channel_id=1, source_target_pairs={{0,16},{16,0},{32,48},{48,32},{64,80},{80,64},{96,112},{112,96},{1... | collective-permute-start | bytes 3145736 | tf_op jit(solution)/shard_map/ppermute | solution.py:198
  298.3 16.4 %collective-permute-start.36 = (f32[40,128]{1,0:T(8,128)S(1)}, f32[40,128]{1,0:T(8,128)S(1)}, u32[]{:S(2)}, u32[]{:S(2)}) collective-permute-start(f32[40,128]{1,0:T(8,128)S(1)} %fusion.86), channel_id=1, source_target_pairs={{0,16},{16,0},{32,48},{48,32},{64,80},{80,64},{96,112},{112,96},{1... | collective-permute-start | bytes 61448 | tf_op jit(solution)/shard_map/ppermute | solution.py:198
  301.6 50.9 %collective-permute-start.17 = (bf16[512,2048]{1,0:T(8,128)(2,1)}, bf16[512,2048]{1,0:T(8,128)(2,1)}, u32[]{:S(2)}, u32[]{:S(2)}) collective-permute-start(bf16[512,2048]{1,0:T(8,128)(2,1)} %slice.407), channel_id=1, source_target_pairs={{0,1},{1,0},{2,3},{3,2},{4,5},{5,4},{6,7},{7,6},{8,9},{9,8},{10,11... | collective-permute-start | bytes 6291464 | tf_op jit(solution)/shard_map/ppermute | solution.py:184
  314.6 41.4 %collective-permute-start.16 = (bf16[512,2048]{1,0:T(8,128)(2,1)S(1)}, bf16[512,2048]{1,0:T(8,128)(2,1)}, u32[]{:S(2)}, u32[]{:S(2)}) collective-permute-start(bf16[512,2048]{1,0:T(8,128)(2,1)S(1)} %slice.408), channel_id=1, source_target_pairs={{0,1},{1,0},{2,3},{3,2},{4,5},{5,4},{6,7},{7,6},{8,9},{9,8},{10,11... | collective-permute-start | bytes 6291464 | tf_op jit(solution)/shard_map/ppermute | solution.py:184
  319.3 13.9 %collective-permute-start.24 = (bf16[1,2,1,256,512]{4,3,2,1,0:T(8,128)(2,1)}, bf16[1,2,1,256,512]{4,3,2,1,0:T(8,128)(2,1)}, u32[]{:S(2)}, u32[]{:S(2)}) collective-permute-start(bf16[1,2,1,256,512]{4,3,2,1,0:T(8,128)(2,1)} %constant_dynamic-slice_fusion.7), channel_id=1, source_target_pairs={{0,64},{16,80},{32,96},{48,112},{64,0},{80,16},{96,32},{112,48},{1... | collective-permute-start | bytes 1572872 | tf_op jit(solution)/shard_map/ppermute | solution.py:198
  343.8 25.3 %collective-permute-start.39 = (f32[10,2048]{1,0:T(8,128)S(1)}, f32[10,2048]{1,0:T(8,128)}, u32[]{:S(2)}, u32[]{:S(2)}) collective-permute-start(f32[10,2048]{1,0:T(8,128)S(1)} %add.451), channel_id=1, source_target_pairs={{0,12},{2,14},{4,8},{6,10},{8,4},{10,6},{12,0},{14,2},{1,13},{3,15... | collective-permute-start | bytes 245768 | tf_op jit(solution)/shard_map/ppermute | solution.py:428
  347.1 15.2 %all-to-all-start.4 = ((bf16[8,32,896]{2,1,0:T(8,128)(2,1)}), bf16[8,32,896]{2,1,0:T(8,128)(2,1)S(1)}, u32[]{:S(2)}, u32[]{:S(2)}) async-start(bf16[8,32,896]{2,1,0:T(8,128)(2,1)} %pad_maximum_fusion.13), calls=%async_computation.4 | async-start | bytes 917504 | tf_op jit(solution)/shard_map/all_to_all | solution.py:368
  362.3 64.7 %all-to-all-start.3 = ((bf16[8,128,2048]{2,1,0:T(8,128)(2,1)}), bf16[8,128,2048]{2,1,0:T(8,128)(2,1)}, u32[]{:S(2)}, u32[]{:S(2)}) async-start(bf16[8,128,2048]{2,1,0:T(8,128)(2,1)} %pad_maximum_fusion.1), calls=%async_computation.3 | async-start | bytes 8388608 | tf_op jit(solution)/shard_map/all_to_all | solution.py:394
  (91 other events, 870.9 us)
